TPU v7x, 32 devices: a whole 2x2x4 slice. The times are simulated.
32 devices in a mesh: col: 16 (over z, y, core), seq: 2 (over x).
Axes of the slice: x: 2, y: 2, z: 4, core: 2. Of those that a mesh axis runs over, the one named last changes fastest.
Arguments:
- history_items: int32 [16, 1024], P(None, 'seq'), may hold values from 0 to 65535
- lengths: int32 [16], replicated, may hold values from 64 to 1024, as said below
- item_table: float32 [512, 65536], P('col'), may hold values from -4 to 4
- input_weight: bfloat16 [512, 2048], replicated, may hold values from -0.25 to 0.25
- output_weight: bfloat16 [512, 512], replicated, may hold values from -0.25 to 0.25
- output_cotangent: bfloat16 [16, 1024, 512], P('col', 'seq'), may hold values from -6 to 6
Outputs:
- layer_output: bfloat16 [16, 1024, 512], P('col', 'seq')
- table_gradient: float32 [512, 65536], P('col', 'seq')
Inputs may be any that keep to these rules, and one draw needn't show every extreme that they name: `lengths`: in every draw one history has exactly 1024 items.
All inputs are finite; a program needn't handle non-finite values.
Results may differ from a plain program's by a relative error of at most 0.0077.
Values may be sent and summed in bfloat16 or wider, within the bound.
A program may use at most 128 MiB of HBM per device.

v0:
```python
import jax
import jax.numpy as jnp
from jax import lax
from jax.experimental import pallas as pl
from jax.experimental.pallas import tpu as pltpu
from jax.sharding import PartitionSpec as P

H = 8
DH = 64
LEN = 1024


norm_epsilon = 1e-05


LANES = 128
COPIES = 8
VMEM_BYTES = 58 * 1024 * 1024


def packed_place(items, feat):
    groups = LANES // feat
    row = (items // (LANES * groups)) * LANES + items % LANES
    slot = (items // LANES) % groups
    return row, slot


def lookup_kernel(rows_ref, slot_ref, table_ref, out_ref, packed, picked):
    feat, table_cols = table_ref.shape
    users, _, seq_rows = slot_ref.shape
    groups = LANES // feat
    span = LANES * groups

    def pack(block, carry):
        base = pl.multiple_of(block * span, span)
        parts = [table_ref[:, pl.ds(base + g * LANES, LANES)] for g in range(groups)]
        turned = jnp.concatenate(parts, axis=0).T
        packed[pl.ds(pl.multiple_of(block * LANES, LANES), LANES), :] = turned
        return carry

    lax.fori_loop(0, table_cols // span, pack, 0, unroll=2)

    def one_user(user, carry):
        def pick(step, inner):
            base = pl.multiple_of(step * 32, 32)
            for offset in range(32):
                row = rows_ref[user, base + offset]
                picked[pl.ds(base + offset, 1), :] = packed[pl.ds(row, 1), :]
            return inner

        lax.fori_loop(0, seq_rows // 32, pick, 0)
        for part in range(seq_rows // LANES):
            turned = picked[pl.ds(part * LANES, LANES), :].T
            slot = slot_ref[user, :, pl.ds(part * LANES, LANES)]
            total = jnp.zeros((feat, LANES), jnp.float32)
            for g in range(groups):
                total = jnp.where(slot == g, turned[g * feat : (g + 1) * feat, :], total)
            out_ref[user, :, pl.ds(part * LANES, LANES)] = total.astype(out_ref.dtype)
        return carry

    lax.fori_loop(0, users, one_user, 0)


def lookup(items, item_table):
    feat, table_cols = item_table.shape
    users, seq_rows = items.shape
    row, slot = packed_place(items, feat)
    return pl.pallas_call(
        lookup_kernel,
        out_shape=jax.ShapeDtypeStruct((users, feat, seq_rows), jnp.bfloat16),
        in_specs=[
            pl.BlockSpec(memory_space=pltpu.SMEM),
            pl.BlockSpec(memory_space=pltpu.VMEM),
            pl.BlockSpec(memory_space=pltpu.VMEM),
        ],
        out_specs=pl.BlockSpec(memory_space=pltpu.VMEM),
        scratch_shapes=[
            pltpu.VMEM((table_cols * feat // LANES, LANES), jnp.float32),
            pltpu.VMEM((seq_rows, LANES), jnp.float32),
        ],
        compiler_params=pltpu.CompilerParams(vmem_limit_bytes=VMEM_BYTES),
        name="lookup",
    )(row, slot[:, None], item_table)


def scatter_kernel(rows_ref, slot_ref, grad_ref, out_ref, placed, *sums):
    feat, owned = out_ref.shape
    blocks, _, seq_rows = slot_ref.shape
    groups = LANES // feat
    span = LANES * groups

    def clear(step, carry):
        at = pl.ds(pl.multiple_of(step * LANES, LANES), LANES)
        for total in sums:
            total[at, :] = jnp.zeros((LANES, LANES), jnp.float32)
        return carry

    lax.fori_loop(0, owned // span, clear, 0)

    def one_block(block, carry):
        for part in range(seq_rows // LANES):
            grad = grad_ref[block, :, pl.ds(part * LANES, LANES)].astype(jnp.float32)
            slot = slot_ref[block, :, pl.ds(part * LANES, LANES)]
            spread = jnp.concatenate(
                [jnp.where(slot == g, grad, 0.0) for g in range(groups)], axis=0
            )
            placed[pl.ds(part * LANES, LANES), :] = spread.T

        def add(step, inner):
            base = pl.multiple_of(step * 4 * COPIES, 4 * COPIES)
            for quarter in range(4):
                first = base + quarter * COPIES
                rows = [rows_ref[block, first + n] for n in range(COPIES)]
                news = [
                    sums[n][pl.ds(rows[n], 1), :] + placed[pl.ds(first + n, 1), :]
                    for n in range(COPIES)
                ]
                for n in range(COPIES):
                    sums[n][pl.ds(rows[n], 1), :] = news[n]
            return inner

        lax.fori_loop(0, seq_rows // (4 * COPIES), add, 0)
        return carry

    lax.fori_loop(0, blocks, one_block, 0)

    def unpack(step, carry):
        at = pl.ds(pl.multiple_of(step * LANES, LANES), LANES)
        total = sums[0][at, :]
        for other in sums[1:]:
            total = total + other[at, :]
        turned = total.T
        base = pl.multiple_of(step * span, span)
        for g in range(groups):
            out_ref[:, pl.ds(base + g * LANES, LANES)] = turned[g * feat : (g + 1) * feat, :]
        return carry

    lax.fori_loop(0, owned // span, unpack, 0, unroll=2)


def scatter(items, grads, owned, seq_index):
    feat = grads.shape[1]
    local = items % owned
    row, slot = packed_place(local, feat)
    slot = jnp.where(items // owned == seq_index, slot, -1)
    packed_rows = owned * feat // LANES
    return pl.pallas_call(
        scatter_kernel,
        out_shape=jax.ShapeDtypeStruct((feat, owned), jnp.float32),
        in_specs=[
            pl.BlockSpec(memory_space=pltpu.SMEM),
            pl.BlockSpec(memory_space=pltpu.VMEM),
            pl.BlockSpec(memory_space=pltpu.VMEM),
        ],
        out_specs=pl.BlockSpec(memory_space=pltpu.VMEM),
        scratch_shapes=[pltpu.VMEM((grads.shape[2], LANES), jnp.float32)]
        + [pltpu.VMEM((packed_rows, LANES), jnp.float32)] * COPIES,
        compiler_params=pltpu.CompilerParams(vmem_limit_bytes=VMEM_BYTES),
        name="scatter",
    )(row, slot[:, None], grads)


BLOCK = 256
F32 = jnp.float32
BF16 = jnp.bfloat16


def dot(left, right):
    return jnp.dot(left, right, preferred_element_type=F32)


def dot_last(left, right):
    return lax.dot_general(left, right, (((1,), (1,)), ((), ())), preferred_element_type=F32)


def turn(block):
    return block.astype(F32).T


def column_stats(block):
    average = jnp.mean(block, axis=0, keepdims=True)
    centered = block - average
    variance = jnp.mean(centered * centered, axis=0, keepdims=True)
    return centered, lax.rsqrt(variance + norm_epsilon)


def norm_back(normed, scale, grad):
    along = jnp.mean(grad * normed, axis=0, keepdims=True)
    return scale * (grad - jnp.mean(grad, axis=0, keepdims=True) - normed * along)


def sigmoid(block):
    return 0.5 + 0.5 * jnp.tanh(0.5 * block)


def layer_kernel(
    place_ref, own_ref, peer_ref, in_turned_ref, in_ref, out_turned_ref, out_w_ref, cot_ref,
    out_ref, entry_ref, partial_ref,
    normed, act, slope, act_peer, slope_peer, query_rows, att, scale, gated, grad_cols, grad_rows,
    point, bend, point_peer, bend_peer, pre_grad, pre_grad_peer, query_grad,
):
    hidden, rows = own_ref.shape
    seq_index = place_ref[0]
    length = place_ref[1]
    first = seq_index * rows
    score_scale = DH ** (-0.5)
    length_scale = 1.0 / LEN
    lane_pos = lax.broadcasted_iota(jnp.int32, (1, rows), 1)
    valid = lane_pos + first < length
    valid_peer = lane_pos < length
    has_peer = seq_index == 1

    def normalize(ref):
        def chunk(step, carry):
            at = pl.ds(pl.multiple_of(step * LANES, LANES), LANES)
            centered, inverse = column_stats(ref[:, at].astype(F32))
            normed[:, at] = (centered * inverse).astype(BF16)
            return carry

        lax.fori_loop(0, rows // LANES, chunk, 0)

    def project(from_row, to_row, count, act_out, slope_out, keep):
        def tile(step, carry):
            source = pl.ds(pl.multiple_of(from_row + step * BLOCK, BLOCK), BLOCK)
            target = pl.ds(pl.multiple_of(to_row + step * BLOCK, BLOCK), BLOCK)
            pre = dot(in_turned_ref[source, :], normed[...])
            sig = sigmoid(pre)
            result = pre * sig
            if keep is not None:
                result = jnp.where(keep, result, 0.0)
            act_out[target, :] = result.astype(BF16)
            slope_out[target, :] = sig * (1.0 + pre * (1.0 - sig))
            return carry

        lax.fori_loop(0, count // BLOCK, tile, 0)

    normalize(own_ref)
    project(0, 0, hidden, act, slope, None)
    project(hidden, hidden, hidden, act, slope, valid)
    project(2 * hidden, 2 * hidden, 2 * hidden, act, slope, None)

    @pl.when(has_peer)
    def _():
        normalize(peer_ref)
        project(hidden, 0, hidden, act_peer, slope_peer, valid_peer)
        project(3 * hidden, hidden, hidden, act_peer, slope_peer, None)

    def head_rows(start, head):
        return pl.ds(pl.multiple_of(start + head * DH, DH), DH)

    def weigh(scores):
        scaled = scores * score_scale
        sig = sigmoid(scaled)
        silu = scaled * sig
        return silu * length_scale, (sig + silu * (1.0 - sig)) * length_scale

    below = lax.broadcasted_iota(jnp.int32, (BLOCK, BLOCK), 1) <= lax.broadcasted_iota(
        jnp.int32, (BLOCK, BLOCK), 0
    )
    blocks = rows // BLOCK

    def forward(head, carry):
        query_rows[head] = turn(act[head_rows(2 * hidden, head), :]).astype(BF16)
        for i in range(blocks):
            at_i = pl.ds(i * BLOCK, BLOCK)
            query = query_rows[head, at_i, :]
            total = jnp.zeros((DH, BLOCK), F32)
            for j in range(i + 1):
                at_j = pl.ds(j * BLOCK, BLOCK)
                weight, curve = weigh(dot(query, act[head_rows(3 * hidden, head), at_j]))
                if i == j:
                    weight = jnp.where(below, weight, 0.0)
                    curve = jnp.where(below, curve, 0.0)
                weight = weight.astype(BF16)
                point[head, at_i, at_j] = weight
                bend[head, at_i, at_j] = curve.astype(BF16)
                total += dot_last(act[head_rows(hidden, head), at_j], weight)
            att[head_rows(0, head), at_i] = total

        @pl.when(has_peer)
        def _():
            for i in range(blocks):
                at_i = pl.ds(i * BLOCK, BLOCK)
                query = query_rows[head, at_i, :]
                weight, curve = weigh(dot(query, act_peer[head_rows(hidden, head), :]))
                weight = weight.astype(BF16)
                point_peer[head, at_i, :] = weight
                bend_peer[head, at_i, :] = curve.astype(BF16)
                att[head_rows(0, head), at_i] += dot_last(act_peer[head_rows(0, head), :], weight)

        return carry

    lax.fori_loop(0, H, forward, 0)

    def gate(step, carry):
        at = pl.ds(pl.multiple_of(step * LANES, LANES), LANES)
        centered, inverse = column_stats(att[:, at])
        normed_att = centered * inverse
        att[:, at] = normed_att
        scale[:, at] = inverse
        gated[:, at] = (normed_att * act[0:hidden, at].astype(F32)).astype(BF16)
        return carry

    lax.fori_loop(0, rows // LANES, gate, 0)

    def mix(step, carry):
        at = pl.ds(pl.multiple_of(step * LANES, LANES), LANES)
        mixed = dot(out_turned_ref[...], gated[:, at]) + own_ref[:, at].astype(F32)
        base = first + step * LANES
        row_valid = lax.broadcasted_iota(jnp.int32, (LANES, hidden), 0) + base < length
        out_ref[at, :] = jnp.where(row_valid, mixed.T, 0.0).astype(BF16)
        cot = jnp.where(row_valid, cot_ref[at, :].astype(F32), 0.0).astype(BF16)
        gated_grad = dot_last(out_w_ref[...], cot)
        normed_att = att[:, at]
        pre_grad[0:hidden, at] = (gated_grad * normed_att * slope[0:hidden, at]).astype(BF16)
        normed_grad = gated_grad * act[0:hidden, at].astype(F32)
        att_grad = norm_back(normed_att, scale[:, at], normed_grad)
        grad_cols[:, at] = att_grad.astype(BF16)
        return carry

    lax.fori_loop(0, rows // LANES, mix, 0)

    def backward(head, carry):
        grad_rows[...] = turn(grad_cols[head_rows(0, head), :]).astype(BF16)
        query_grad[...] = jnp.zeros_like(query_grad)

        @pl.when(has_peer)
        def _():
            value_total = jnp.zeros((DH, rows), F32)
            key_total = jnp.zeros((DH, rows), F32)
            for i in range(blocks):
                at_i = pl.ds(i * BLOCK, BLOCK)
                weight_grad = dot(grad_rows[at_i, :], act_peer[head_rows(0, head), :])
                score_grad = (weight_grad * bend_peer[head, at_i, :].astype(F32)).astype(BF16)
                value_total += dot(grad_cols[head_rows(0, head), at_i], point_peer[head, at_i, :])
                key_total += dot(act[head_rows(2 * hidden, head), at_i], score_grad)
                query_grad[:, at_i] = dot_last(act_peer[head_rows(hidden, head), :], score_grad)
            value_total = jnp.where(valid_peer, value_total, 0.0)
            pre_grad_peer[head_rows(0, head), :] = (
                value_total * slope_peer[head_rows(0, head), :]
            ).astype(BF16)
            pre_grad_peer[head_rows(hidden, head), :] = (
                key_total * score_scale * slope_peer[head_rows(hidden, head), :]
            ).astype(BF16)

        value_parts = [jnp.zeros((DH, BLOCK), F32) for _ in range(blocks)]
        key_parts = [jnp.zeros((DH, BLOCK), F32) for _ in range(blocks)]
        for i in range(blocks):
            at_i = pl.ds(i * BLOCK, BLOCK)
            for j in range(i + 1):
                at_j = pl.ds(j * BLOCK, BLOCK)
                weight_grad = dot(grad_rows[at_i, :], act[head_rows(hidden, head), at_j])
                score_grad = (weight_grad * bend[head, at_i, at_j].astype(F32)).astype(BF16)
                value_parts[j] += dot(grad_cols[head_rows(0, head), at_i], point[head, at_i, at_j])
                key_parts[j] += dot(act[head_rows(2 * hidden, head), at_i], score_grad)
                query_grad[:, at_i] += dot_last(act[head_rows(3 * hidden, head), at_j], score_grad)
        value_total = jnp.where(valid, jnp.concatenate(value_parts, axis=1), 0.0)
        key_total = jnp.concatenate(key_parts, axis=1) * score_scale
        for start, total in (
            (hidden, value_total),
            (2 * hidden, query_grad[...] * score_scale),
            (3 * hidden, key_total),
        ):
            at = head_rows(start, head)
            pre_grad[at, :] = (total * slope[at, :]).astype(BF16)
        return carry

    lax.fori_loop(0, H, backward, 0)

    def leave(step, carry):
        at = pl.ds(pl.multiple_of(step * BLOCK, BLOCK), BLOCK)
        entry_ref[at, :] = dot(in_ref[at, :], pre_grad[...])
        return carry

    lax.fori_loop(0, hidden // BLOCK, leave, 0)

    @pl.when(has_peer)
    def _():
        def leave_peer(step, carry):
            at = pl.ds(pl.multiple_of(step * BLOCK, BLOCK), BLOCK)
            total = dot(in_ref[at, hidden : 2 * hidden], pre_grad_peer[0:hidden, :])
            total += dot(in_ref[at, 3 * hidden :], pre_grad_peer[hidden:, :])
            partial_ref[at, :] = total.astype(BF16)
            return carry

        lax.fori_loop(0, hidden // BLOCK, leave_peer, 0)

    @pl.when(jnp.logical_not(has_peer))
    def _():
        partial_ref[...] = jnp.zeros_like(partial_ref)


def layer(place, own, peer, input_weight, output_weight, cot):
    hidden, rows = own.shape
    vmem = pl.BlockSpec(memory_space=pltpu.VMEM)
    return pl.pallas_call(
        layer_kernel,
        out_shape=(
            jax.ShapeDtypeStruct((rows, hidden), BF16),
            jax.ShapeDtypeStruct((hidden, rows), F32),
            jax.ShapeDtypeStruct((hidden, rows), BF16),
        ),
        in_specs=[pl.BlockSpec(memory_space=pltpu.SMEM)] + [vmem] * 7,
        out_specs=(vmem,) * 3,
        scratch_shapes=[
            pltpu.VMEM((hidden, rows), BF16),
            pltpu.VMEM((4 * hidden, rows), BF16),
            pltpu.VMEM((4 * hidden, rows), F32),
            pltpu.VMEM((2 * hidden, rows), BF16),
            pltpu.VMEM((2 * hidden, rows), F32),
            pltpu.VMEM((H, rows, DH), BF16),
            pltpu.VMEM((hidden, rows), F32),
            pltpu.VMEM((1, rows), F32),
            pltpu.VMEM((hidden, rows), BF16),
            pltpu.VMEM((hidden, rows), BF16),
            pltpu.VMEM((rows, DH), BF16),
            pltpu.VMEM((H, rows, rows), BF16),
            pltpu.VMEM((H, rows, rows), BF16),
            pltpu.VMEM((H, rows, rows), BF16),
            pltpu.VMEM((H, rows, rows), BF16),
            pltpu.VMEM((4 * hidden, rows), BF16),
            pltpu.VMEM((2 * hidden, rows), BF16),
            pltpu.VMEM((DH, rows), F32),
        ],
        compiler_params=pltpu.CompilerParams(vmem_limit_bytes=VMEM_BYTES),
        name="layer",
    )(place, own, peer, input_weight.T, input_weight, output_weight.T, output_weight, cot)


def finish_kernel(place_ref, own_ref, entry_ref, extra_ref, cot_ref, out_ref):
    hidden, rows = own_ref.shape
    first = place_ref[0] * rows
    length = place_ref[1]

    def chunk(step, carry):
        at = pl.ds(pl.multiple_of(step * LANES, LANES), LANES)
        centered, inverse = column_stats(own_ref[:, at].astype(F32))
        grad = entry_ref[:, at] + extra_ref[:, at].astype(F32)
        back = norm_back(centered * inverse, inverse, grad)
        lane_valid = (
            lax.broadcasted_iota(jnp.int32, (1, LANES), 1) + first + step * LANES < length
        )
        cot = jnp.where(lane_valid, turn(cot_ref[at, :]), 0.0)
        out_ref[:, at] = (cot + back).astype(BF16)
        return carry

    lax.fori_loop(0, rows // LANES, chunk, 0)


def finish(place, own, entry, extra, cot):
    vmem = pl.BlockSpec(memory_space=pltpu.VMEM)
    return pl.pallas_call(
        finish_kernel,
        out_shape=jax.ShapeDtypeStruct(own.shape, BF16),
        in_specs=[pl.BlockSpec(memory_space=pltpu.SMEM)] + [vmem] * 4,
        out_specs=vmem,
        compiler_params=pltpu.CompilerParams(vmem_limit_bytes=VMEM_BYTES),
        name="finish",
    )(place, own, entry, extra, cot)


def per_device(history_items, lengths, item_table, input_weight, output_weight, output_cotangent):
    user_count, seq_rows = history_items.shape
    feat_cols = item_table.shape[0]
    col_index = lax.axis_index("col")
    seq_index = lax.axis_index("seq")
    chosen = jnp.arange(lengths.shape[0], dtype=jnp.int32) == col_index
    length = jnp.sum(jnp.where(chosen, lengths, 0))
    place = jnp.stack([seq_index, length]).astype(jnp.int32)
    every_item = lax.all_gather(history_items, "seq", axis=0, tiled=True)
    looked = lookup(history_items, item_table)
    own = lax.all_to_all(looked, "col", split_axis=0, concat_axis=1, tiled=True)[0]
    peer = lax.ppermute(own, "seq", [(0, 1)])
    cot = output_cotangent[0]
    layer_output, entry, partial = layer(place, own, peer, input_weight, output_weight, cot)
    extra = lax.ppermute(partial, "seq", [(1, 0)])
    input_grad = finish(place, own, entry, extra, cot)
    back = lax.all_to_all(
        input_grad.reshape(user_count, feat_cols, seq_rows),
        "col",
        split_axis=0,
        concat_axis=0,
        tiled=True,
    )
    every_grad = lax.all_gather(back, "seq", axis=0, tiled=True)
    owned_rows = item_table.shape[1] // lax.axis_size("seq")
    table_gradient = scatter(every_item, every_grad, owned_rows, seq_index)
    return (layer_output[None], table_gradient)


def solution(mesh):
    in_specs = (P(None, "seq"), P(), P("col", None), P(), P(), P("col", "seq", None))
    out_specs = (P("col", "seq", None), P("col", "seq"))
    return jax.shard_map(
        per_device, mesh=mesh, in_specs=in_specs, out_specs=out_specs, check_vma=False
    )
```

profile of v0, /device:TPU:0, one launch (start us, length us, event | category | flops | bytes accessed | tf_op | source)
XLA Modules:
  0.0 244.5 jit_solution(5697577388732299251)
XLA Ops:
  7.2 0.0 all-gather.2.cloned.1.call-start
  7.2 1.4 add_select_fusion.6
  8.6 0.6 broadcast_in_dim.16.slot_ref
  9.3 0.0 copy-start
  9.3 33.4 %lookup.1 = bf16[16,32,512]{2,1,0:T(8,128)(2,1)} custom-call(s32[16,512]{1,0:T(8,128)} %get-tuple-element.11.rows_ref, s32[16,1,512]{2,1,0:T(1,128)} %broadcast_in_dim.16.slot_ref, f32[32,65536]{1,0:T(8,128)} %table_ref.1), custom_call_target="tpu_custom_call" | custom-call | tf_op jit(solution)/shard_map/lookup/pallas_call | solution.py:68
  42.7 0.0 copy-start.2
  42.7 0.0 copy-start.5
  42.7 22.0 %all_to_all.14 = bf16[16,32,512]{2,1,0:T(8,128)(2,1)S(1)} all-to-all(bf16[16,32,512]{2,1,0:T(8,128)(2,1)} %lookup.1), channel_id=1, replica_groups=mesh['col'=16,'seq'=2] {'col'}, dimensions={0} | all-to-all | bytes 1048576 | tf_op jit(solution)/shard_map/all_to_all | solution.py:472
  64.7 0.0 copy-start.1
  64.7 4.2 %collective-permute-start = (bf16[512,512]{1,0:T(8,128)(2,1)S(1)}, bf16[512,512]{1,0:T(8,128)(2,1)}, u32[]{:S(2)}, u32[]{:S(2)}) collective-permute-start(bf16[512,512]{1,0:T(8,128)(2,1)S(1)} %bitcast.9), channel_id=1, source_target_pairs={{0,1},{2,3},{4,5},{6,7},{8,9},{10,11},{12,13},{14,15},{16,17},{18,... | collective-permute-start | bytes 1572872 | tf_op jit(solution)/shard_map/ppermute | solution.py:473
  68.9 0.0 copy-done
  68.9 2.5 %copy.10 = bf16[512,2048]{0,1:T(8,128)(2,1)} copy(bf16[512,2048]{1,0:T(8,128)(2,1)S(1)} %copy-done) | data formatting | bytes 4194304 | tf_op args[3]
  71.4 0.0 copy-done.2
  71.4 1.0 copy.11
  72.4 0.0 copy-done.5
  72.4 0.6 fusion.16
  73.0 1.3 pad_add_fusion.place_ref
  74.3 5.2 %collective-permute-done.peer_ref = bf16[512,512]{1,0:T(8,128)(2,1)} collective-permute-done((bf16[512,512]{1,0:T(8,128)(2,1)S(1)}, bf16[512,512]{1,0:T(8,128)(2,1)}, u32[]{:S(2)}, u32[]{:S(2)}) %collective-permute-start) | collective-permute-done | bytes 524320 | tf_op jit(solution)/shard_map/ppermute | solution.py:473
  79.4 0.0 copy-done.1
  79.4 0.0 copy-start.4
  79.4 26.8 %layer.1 = (bf16[512,512]{1,0:T(8,128)(2,1)}, f32[512,512]{1,0:T(8,128)}, bf16[512,512]{1,0:T(8,128)(2,1)}) custom-call(s32[2]{0:T(128)} %pad_add_fusion.place_ref, bf16[512,512]{1,0:T(8,128)(2,1)} %bitcast.10, bf16[512,512]{1,0:T(8,128)(2,1)} %collective-permute-done.peer_ref, bf16[2048,512]{1,0:T(8,128)(2,1)} %bitcast.8, bf16[512,2048]{1,0:T(8,128)(2,1)} %in_ref.1, ...), custom_call_target="tpu_custom_call" | custom-call | tf_op jit(solution)/shard_map/layer/pallas_call | solution.py:396
  106.2 1.3 collective-permute-start.1
  107.5 30.3 %collective-permute-done.1.extra_ref = bf16[512,512]{1,0:T(8,128)(2,1)S(1)} collective-permute-done((bf16[512,512]{1,0:T(8,128)(2,1)}, bf16[512,512]{1,0:T(8,128)(2,1)S(1)}, u32[]{:S(2)}, u32[]{:S(2)}) %collective-permute-start.1) | collective-permute-done | bytes 524320 | tf_op jit(solution)/shard_map/ppermute | solution.py:476
  137.8 0.0 copy-start.3
  137.8 0.8 copy-done.3
  138.6 3.8 %finish.1 = bf16[512,512]{1,0:T(8,128)(2,1)} custom-call(s32[2]{0:T(128)} %pad_add_fusion.place_ref, bf16[512,512]{1,0:T(8,128)(2,1)} %bitcast.11, f32[512,512]{1,0:T(8,128)} %get-tuple-element.6.entry_ref, bf16[512,512]{1,0:T(8,128)(2,1)} %copy-done.3, bf16[512,512]{1,0:T(8,128)(2,1)} %bitcast.15), custom_call_target="tpu_custom_call" | custom-call | tf_op jit(solution)/shard_map/finish/pallas_call | solution.py:452
  142.4 19.3 %all_to_all.15 = bf16[16,32,512]{2,1,0:T(8,128)(2,1)} all-to-all(bf16[16,32,512]{2,1,0:T(8,128)(2,1)} %bitcast.12), channel_id=1, replica_groups=mesh['col'=16,'seq'=2] {'col'}, dimensions={0} | all-to-all | bytes 1048576 | tf_op jit(solution)/shard_map/all_to_all | solution.py:478
  161.6 0.0 all-gather.2.cloned.1.call-update
  161.6 0.0 copy-done.4
  161.7 4.6 %all_gather.6 = s32[32,512]{1,0:T(8,128)S(1)} all-gather(s32[16,512]{1,0:T(8,128)S(1)} %copy-done.4), channel_id=1, replica_groups=mesh['col'=16,'seq'=2] {'seq'}, dimensions={0}, use_global_device_ids=true | all-gather | bytes 98304 | tf_op jit(solution)/shard_map/all_gather | solution.py:470
  166.2 0.8 fusion.5
  167.0 0.7 broadcast_in_dim.18.slot_ref
  167.7 13.9 %all-gather.2.cloned.1.call-done.grad_ref = bf16[32,32,512]{2,1,0:T(8,128)(2,1)} async-done(((bf16[16,32,512]{2,1,0:T(8,128)(2,1)}), bf16[32,32,512]{2,1,0:T(8,128)(2,1)}) %all-gather.2.cloned.1.call-update) | async-done | bytes 1048592 | tf_op jit(solution)/shard_map/all_gather | solution.py:485
  181.6 56.1 %scatter.1 = f32[32,32768]{1,0:T(8,128)} custom-call(s32[32,512]{1,0:T(8,128)} %get-tuple-element.9.rows_ref, s32[32,1,512]{2,1,0:T(1,128)} %broadcast_in_dim.18.slot_ref, bf16[32,32,512]{2,1,0:T(8,128)(2,1)} %all-gather.2.cloned.1.call-done.grad_ref), custom_call_target="tpu_custom_call" | custom-call | tf_op jit(solution)/shard_map/scatter/pallas_call | solution.py:147
Async XLA Ops:
  7.2 174.4 %all-gather.2.cloned.1.call-start = ((), (), s32[]{:S(2)}) async-start(), calls=%async_computation.2 | async-start | bytes 1572864 | tf_op jit(solution)/shard_map/all_gather | solution.py:485
  9.3 59.6 %copy-start = (bf16[512,2048]{1,0:T(8,128)(2,1)S(1)}, bf16[512,2048]{1,0:T(8,128)(2,1)}, u32[]{:S(2)}) copy-start(bf16[512,2048]{1,0:T(8,128)(2,1)} %in_ref.1) | copy-start | bytes 6291460
  42.7 28.7 %copy-start.2 = (bf16[512,512]{1,0:T(8,128)(2,1)S(1)}, bf16[512,512]{1,0:T(8,128)(2,1)}, u32[]{:S(2)}) copy-start(bf16[512,512]{1,0:T(8,128)(2,1)} %out_w_ref.1) | copy-start | bytes 1572868
  42.7 29.7 %copy-start.5 = (s32[16]{0:T(128)S(1)}, s32[16]{0:T(128)}, u32[]{:S(2)}) copy-start(s32[16]{0:T(128)} %param.7) | copy-start | bytes 196
  64.7 14.7 %copy-start.1 = (bf16[16,32,512]{2,1,0:T(8,128)(2,1)}, bf16[16,32,512]{2,1,0:T(8,128)(2,1)S(1)}, u32[]{:S(2)}) copy-start(bf16[16,32,512]{2,1,0:T(8,128)(2,1)S(1)} %all_to_all.14) | copy-start | bytes 1572868
  64.7 14.7 %collective-permute-start = (bf16[512,512]{1,0:T(8,128)(2,1)S(1)}, bf16[512,512]{1,0:T(8,128)(2,1)}, u32[]{:S(2)}, u32[]{:S(2)}) collective-permute-start(bf16[512,512]{1,0:T(8,128)(2,1)S(1)} %bitcast.9), channel_id=1, source_target_pairs={{0,1},{2,3},{4,5},{6,7},{8,9},{10,11},{12,13},{14,15},{16,17},{18,... | collective-permute-start | bytes 1572872 | tf_op jit(solution)/shard_map/ppermute | solution.py:473
  79.4 82.2 %copy-start.4 = (s32[16,512]{1,0:T(8,128)S(1)}, s32[16,512]{1,0:T(8,128)}, u32[]{:S(2)}) copy-start(s32[16,512]{1,0:T(8,128)} %param.6) | copy-start | bytes 98308
  106.2 31.6 %collective-permute-start.1 = (bf16[512,512]{1,0:T(8,128)(2,1)}, bf16[512,512]{1,0:T(8,128)(2,1)S(1)}, u32[]{:S(2)}, u32[]{:S(2)}) collective-permute-start(bf16[512,512]{1,0:T(8,128)(2,1)} %get-tuple-element.7), channel_id=1, source_target_pairs={{1,0},{3,2},{5,4},{7,6},{9,8},{11,10},{13,12},{15,14},{17,16},{19,... | collective-permute-start | bytes 1572872 | tf_op jit(solution)/shard_map/ppermute | solution.py:476
  137.8 0.8 copy-start.3
Sparse Core Ops, SparseCore 0:
  161.8 19.7 all-gather.1
where the time goes:
time: 245 us
  Pallas kernels  120 us (49%)
  waiting for transfers between devices  49.3 us (20%)
  blocking collectives  45.8 us (19%)
  between operations  14.1 us (6%)
  local copies, waits for them, and re-layouts  5.59 us (2%)
  starting transfers between devices  5.5 us (2%)
  other arithmetic  4.1 us (2%)
    pallas_call x1, Pallas kernels, scatter(): pl.pallas_call(scatter_kernel, out_shape=jax.ShapeDtypeStruct((feat, owne...  56.1 us
    pallas_call x1, Pallas kernels, lookup(): pl.pallas_call(lookup_kernel, out_shape=jax.ShapeDtypeStruct((users, feat...  33.4 us
    ppermute x1, waiting for transfers between devices, per_device(): extra = lax.ppermute(partial, 'seq', [(1, 0)])  30.3 us
    pallas_call x1, Pallas kernels, layer(): pl.pallas_call(layer_kernel, out_shape=(jax.ShapeDtypeStruct((rows, hidde...  26.8 us
    all_to_all x1, blocking collectives, per_device(): lax.all_to_all(looked, 'col', split_axis=0, concat_axis=1, tiled=True)[0]  22 us
    all_to_all x1, blocking collectives, per_device(): lax.all_to_all(input_grad.reshape(user_count, feat_cols, seq_rows), 'col'...  19.3 us
    all_gather x1, waiting for transfers between devices, per_device(): every_grad = lax.all_gather(back, 'seq', axis=0, tiled=True)  13.9 us
    ppermute x1, waiting for transfers between devices, per_device(): peer = lax.ppermute(own, 'seq', [(0, 1)])  5.16 us
  transfers between devices with their start and end apart: 3, of which 3 were waited for; matrix products, arithmetic and copies ran while one was open for 3% of the time, Pallas kernels for 0%

commit v1 on v0

--- a/solution.py
+++ b/solution.py
@@ -14,6 +14,7 @@
 
 
 LANES = 128
+MESH = pl.DeviceIdType.MESH
 COPIES = 8
 VMEM_BYTES = 58 * 1024 * 1024
 
@@ -25,11 +26,29 @@
     return row, slot
 
 
-def lookup_kernel(rows_ref, slot_ref, table_ref, out_ref, packed, picked):
+def lookup_kernel(
+    rows_ref, slot_ref, table_ref, own_ref, peer_ref,
+    packed, picked, slab, own, peer, own_sent, own_got, peer_sent, peer_got,
+):
     feat, table_cols = table_ref.shape
     users, _, seq_rows = slot_ref.shape
     groups = LANES // feat
     span = LANES * groups
+    col = lax.axis_index("col")
+    seq = lax.axis_index("seq")
+    barrier = pltpu.get_barrier_semaphore()
+    halves = lax.axis_size("seq")
+
+    def greet(other, carry):
+        @pl.when(other != col * halves + seq)
+        def _():
+            pl.semaphore_signal(
+                barrier, inc=1, device_id=(other // halves, other % halves), device_id_type=MESH
+            )
+
+        return carry
+
+    lax.fori_loop(0, users * halves, greet, 0)
 
     def pack(block, carry):
         base = pl.multiple_of(block * span, span)
@@ -39,10 +58,33 @@
         return carry
 
     lax.fori_loop(0, table_cols // span, pack, 0, unroll=2)
-
-    def one_user(user, carry):
-        def pick(step, inner):
-            base = pl.multiple_of(step * 32, 32)
+    pl.semaphore_wait(barrier, users * halves - 1)
+
+    def to_own(user, sender):
+        return pltpu.make_async_remote_copy(
+            src_ref=slab.at[user],
+            dst_ref=own.at[sender],
+            send_sem=own_sent.at[user],
+            recv_sem=own_got.at[sender],
+            device_id=(user, seq),
+            device_id_type=MESH,
+        )
+
+    def to_peer(user, sender):
+        return pltpu.make_async_remote_copy(
+            src_ref=slab.at[user],
+            dst_ref=peer.at[sender],
+            send_sem=peer_sent.at[user],
+            recv_sem=peer_got.at[sender],
+            device_id=(user, 1),
+            device_id_type=MESH,
+        )
+
+    def one_user(step, carry):
+        user = lax.rem(col + 1 + step, users)
+
+        def pick(part, inner):
+            base = pl.multiple_of(part * 32, 32)
             for offset in range(32):
                 row = rows_ref[user, base + offset]
                 picked[pl.ds(base + offset, 1), :] = packed[pl.ds(row, 1), :]
@@ -55,35 +97,85 @@
             total = jnp.zeros((feat, LANES), jnp.float32)
             for g in range(groups):
                 total = jnp.where(slot == g, turned[g * feat : (g + 1) * feat, :], total)
-            out_ref[user, :, pl.ds(part * LANES, LANES)] = total.astype(out_ref.dtype)
+            slab[user, :, pl.ds(part * LANES, LANES)] = total.astype(slab.dtype)
+
+        @pl.when(seq == 0)
+        def _():
+            to_peer(user, col).start()
+
+        @pl.when(user != col)
+        def _():
+            to_own(user, col).start()
+
         return carry
 
     lax.fori_loop(0, users, one_user, 0)
+    own_ref[col] = slab[col]
+
+    def collect(step, carry):
+        other = lax.rem(col + 1 + step, users)
+        to_own(other, other).wait_recv()
+        own_ref[other] = own[other]
+        return carry
+
+    lax.fori_loop(0, users - 1, collect, 0)
+
+    @pl.when(seq == 1)
+    def _():
+        def collect_peer(other, carry):
+            to_peer(other, other).wait_recv()
+            return carry
+
+        lax.fori_loop(0, users, collect_peer, 0)
+        peer_ref[...] = peer[...]
+
+    @pl.when(seq == 0)
+    def _():
+        peer_ref[...] = jnp.zeros_like(peer_ref)
+
+    def sent(step, carry):
+        other = lax.rem(col + 1 + step, users)
+        to_own(other, col).wait_send()
+        return carry
+
+    lax.fori_loop(0, users - 1, sent, 0)
+
+    @pl.when(seq == 0)
+    def _():
+        def sent_peer(other, carry):
+            to_peer(other, col).wait_send()
+            return carry
+
+        lax.fori_loop(0, users, sent_peer, 0)
 
 
 def lookup(items, item_table):
     feat, table_cols = item_table.shape
     users, seq_rows = items.shape
     row, slot = packed_place(items, feat)
+    vmem = pl.BlockSpec(memory_space=pltpu.VMEM)
+    slabs = (users, feat, seq_rows)
     return pl.pallas_call(
         lookup_kernel,
-        out_shape=jax.ShapeDtypeStruct((users, feat, seq_rows), jnp.bfloat16),
-        in_specs=[
-            pl.BlockSpec(memory_space=pltpu.SMEM),
-            pl.BlockSpec(memory_space=pltpu.VMEM),
-            pl.BlockSpec(memory_space=pltpu.VMEM),
-        ],
-        out_specs=pl.BlockSpec(memory_space=pltpu.VMEM),
+        out_shape=(jax.ShapeDtypeStruct(slabs, jnp.bfloat16),) * 2,
+        in_specs=[pl.BlockSpec(memory_space=pltpu.SMEM), vmem, vmem],
+        out_specs=(vmem, vmem),
         scratch_shapes=[
             pltpu.VMEM((table_cols * feat // LANES, LANES), jnp.float32),
             pltpu.VMEM((seq_rows, LANES), jnp.float32),
-        ],
-        compiler_params=pltpu.CompilerParams(vmem_limit_bytes=VMEM_BYTES),
+            pltpu.VMEM(slabs, jnp.bfloat16),
+            pltpu.VMEM(slabs, jnp.bfloat16),
+            pltpu.VMEM(slabs, jnp.bfloat16),
+        ]
+        + [pltpu.SemaphoreType.DMA((users,))] * 4,
+        compiler_params=pltpu.CompilerParams(
+            vmem_limit_bytes=VMEM_BYTES, collective_id=0, has_side_effects=True
+        ),
         name="lookup",
     )(row, slot[:, None], item_table)
 
 
-def scatter_kernel(rows_ref, slot_ref, grad_ref, out_ref, placed, *sums):
+def scatter_kernel(rows_ref, count_ref, slot_ref, grad_ref, out_ref, placed, *sums):
     feat, owned = out_ref.shape
     blocks, _, seq_rows = slot_ref.shape
     groups = LANES // feat
@@ -98,13 +190,19 @@
     lax.fori_loop(0, owned // span, clear, 0)
 
     def one_block(block, carry):
-        for part in range(seq_rows // LANES):
-            grad = grad_ref[block, :, pl.ds(part * LANES, LANES)].astype(jnp.float32)
-            slot = slot_ref[block, :, pl.ds(part * LANES, LANES)]
+        count = count_ref[block]
+
+        def place(part, inner):
+            at = pl.ds(pl.multiple_of(part * LANES, LANES), LANES)
+            grad = grad_ref[block, :, at].astype(jnp.float32)
+            slot = slot_ref[block, :, at]
             spread = jnp.concatenate(
                 [jnp.where(slot == g, grad, 0.0) for g in range(groups)], axis=0
             )
-            placed[pl.ds(part * LANES, LANES), :] = spread.T
+            placed[at, :] = spread.T
+            return inner
+
+        lax.fori_loop(0, (count + LANES - 1) // LANES, place, 0)
 
         def add(step, inner):
             base = pl.multiple_of(step * 4 * COPIES, 4 * COPIES)
@@ -119,7 +217,7 @@
                     sums[n][pl.ds(rows[n], 1), :] = news[n]
             return inner
 
-        lax.fori_loop(0, seq_rows // (4 * COPIES), add, 0)
+        lax.fori_loop(0, (count + 4 * COPIES - 1) // (4 * COPIES), add, 0)
         return carry
 
     lax.fori_loop(0, blocks, one_block, 0)
@@ -138,7 +236,7 @@
     lax.fori_loop(0, owned // span, unpack, 0, unroll=2)
 
 
-def scatter(items, grads, owned, seq_index):
+def scatter(items, counts, grads, owned, seq_index):
     feat = grads.shape[1]
     local = items % owned
     row, slot = packed_place(local, feat)
@@ -149,6 +247,7 @@
         out_shape=jax.ShapeDtypeStruct((feat, owned), jnp.float32),
         in_specs=[
             pl.BlockSpec(memory_space=pltpu.SMEM),
+            pl.BlockSpec(memory_space=pltpu.SMEM),
             pl.BlockSpec(memory_space=pltpu.VMEM),
             pl.BlockSpec(memory_space=pltpu.VMEM),
         ],
@@ -157,7 +256,7 @@
         + [pltpu.VMEM((packed_rows, LANES), jnp.float32)] * COPIES,
         compiler_params=pltpu.CompilerParams(vmem_limit_bytes=VMEM_BYTES),
         name="scatter",
-    )(row, slot[:, None], grads)
+    )(row, counts, slot[:, None], grads)
 
 
 BLOCK = 256
@@ -468,9 +567,9 @@
     length = jnp.sum(jnp.where(chosen, lengths, 0))
     place = jnp.stack([seq_index, length]).astype(jnp.int32)
     every_item = lax.all_gather(history_items, "seq", axis=0, tiled=True)
-    looked = lookup(history_items, item_table)
-    own = lax.all_to_all(looked, "col", split_axis=0, concat_axis=1, tiled=True)[0]
-    peer = lax.ppermute(own, "seq", [(0, 1)])
+    own, peer = lookup(history_items, item_table)
+    own = own.reshape(user_count * feat_cols, seq_rows)
+    peer = peer.reshape(user_count * feat_cols, seq_rows)
     cot = output_cotangent[0]
     layer_output, entry, partial = layer(place, own, peer, input_weight, output_weight, cot)
     extra = lax.ppermute(partial, "seq", [(1, 0)])
@@ -483,8 +582,10 @@
         tiled=True,
     )
     every_grad = lax.all_gather(back, "seq", axis=0, tiled=True)
+    starts = seq_rows * jnp.arange(lax.axis_size("seq"), dtype=jnp.int32)
+    counts = jnp.clip(lengths[None, :] - starts[:, None], 0, seq_rows).reshape(-1)
     owned_rows = item_table.shape[1] // lax.axis_size("seq")
-    table_gradient = scatter(every_item, every_grad, owned_rows, seq_index)
+    table_gradient = scatter(every_item, counts, every_grad, owned_rows, seq_index)
     return (layer_output[None], table_gradient)
 
 

time: 245 us -> 215 us (0.88); the launches traced: 245 us -> 212 us
  blocking collectives: 45.8 us -> 29.9 us
  waiting for transfers between devices: 49.3 us -> 39.3 us
  Pallas kernels: 120 us -> 115 us
  starting transfers between devices: 5.5 us -> 1.32 us
    all_to_all x1 -> x0, blocking collectives: 22 us -> none  [per_device(): lax.all_to_all(looked, 'col', split_axis=0, concat_axis=1, tiled=True)[0]]
    pallas_call x1, Pallas kernels: 56.1 us -> 43.8 us  [scatter(): pl.pallas_call(scatter_kernel, out_shape=jax.ShapeDtypeStruct((feat, owne...]
    pallas_call x1, Pallas kernels: 33.4 us -> 41 us  [lookup(): pl.pallas_call(lookup_kernel, out_shape=(jax.ShapeDtypeStruct(slabs, jnp....]
    all_to_all x1, blocking collectives: 19.3 us -> 25.3 us  [per_device(): lax.all_to_all(input_grad.reshape(user_count, feat_cols, seq_rows), 'col'...]
    ppermute x1 -> x0, waiting for transfers between devices: 5.16 us -> none  [per_device(): peer = lax.ppermute(own, 'seq', [(0, 1)])]
    ppermute x1, waiting for transfers between devices: 30.3 us -> 26.1 us  [per_device(): extra = lax.ppermute(partial, 'seq', [(1, 0)])]
    ppermute x1 -> x0, starting transfers between devices: 4.19 us -> none  [per_device(): peer = lax.ppermute(own, 'seq', [(0, 1)])]
    unnamed x14 -> x10, local copies, waits for them, and re-layouts: 4.3 us -> 5.72 us
  transfers between devices with their start and end apart: 3 -> 2, of which waited for: 3 -> 2; matrix products, arithmetic and copies ran while one was open for 3% -> 1% of each run, Pallas kernels for 0% -> 0%
where the time goes in v1:
time: 215 us; the launch traced here: 212 us
  Pallas kernels  115 us (53%)
  waiting for transfers between devices  39.3 us (18%)
  blocking collectives  29.9 us (14%)
  between operations  14.1 us (7%)
  local copies, waits for them, and re-layouts  7.69 us (4%)
  other arithmetic  4.22 us (2%)
    pallas_call x1, Pallas kernels, scatter(): pl.pallas_call(scatter_kernel, out_shape=jax.ShapeDtypeStruct((feat, owne...  43.8 us
    pallas_call x1, Pallas kernels, lookup(): pl.pallas_call(lookup_kernel, out_shape=(jax.ShapeDtypeStruct(slabs, jnp....  41 us
    pallas_call x1, Pallas kernels, layer(): pl.pallas_call(layer_kernel, out_shape=(jax.ShapeDtypeStruct((rows, hidde...  26.8 us
    ppermute x1, waiting for transfers between devices, per_device(): extra = lax.ppermute(partial, 'seq', [(1, 0)])  26.1 us
    all_to_all x1, blocking collectives, per_device(): lax.all_to_all(input_grad.reshape(user_count, feat_cols, seq_rows), 'col'...  25.3 us
    all_gather x1, waiting for transfers between devices, per_device(): every_grad = lax.all_gather(back, 'seq', axis=0, tiled=True)  13.1 us
    unnamed x10, local copies, waits for them, and re-layouts  5.72 us
    all_gather x1, blocking collectives, per_device(): every_item = lax.all_gather(history_items, 'seq', axis=0, tiled=True)  4.58 us
  transfers between devices with their start and end apart: 2, of which 2 were waited for; matrix products, arithmetic and copies ran while one was open for 1% of the time, Pallas kernels for 0%

profile of v1, /device:TPU:0, one launch (start us, length us, event | category | flops | bytes accessed | tf_op | source)
XLA Modules:
  0.0 211.7 jit_solution(14890325332749696460)
XLA Ops:
  7.2 0.0 copy-start
  7.2 0.0 copy-start.3
  7.2 0.0 all-gather.2.cloned.1.call-start
  7.2 1.5 add_select_fusion.6
  8.7 0.6 broadcast_in_dim.18.slot_ref
  9.3 3.9 %copy.10 = bf16[512,2048]{0,1:T(8,128)(2,1)} copy(bf16[512,2048]{1,0:T(8,128)(2,1)} %in_ref.1) | data formatting | bytes 4194304 | tf_op args[3]
  13.3 0.0 copy-done
  13.3 1.0 copy.11
  14.3 0.0 copy-done.3
  14.3 0.7 fusion.16
  14.9 1.2 pad_add_fusion.place_ref
  16.1 41.0 %lookup.1 = (bf16[16,32,512]{2,1,0:T(8,128)(2,1)}, bf16[16,32,512]{2,1,0:T(8,128)(2,1)}) custom-call(s32[16,512]{1,0:T(8,128)} %get-tuple-element.15.rows_ref, s32[16,1,512]{2,1,0:T(1,128)} %broadcast_in_dim.18.slot_ref, f32[32,65536]{1,0:T(8,128)} %table_ref.1), custom_call_target="tpu_custom_call" | custom-call | tf_op jit(solution)/shard_map/lookup/pallas_call | solution.py:158
  57.1 0.0 copy-start.2
  57.1 26.8 %layer.1 = (bf16[512,512]{1,0:T(8,128)(2,1)}, f32[512,512]{1,0:T(8,128)}, bf16[512,512]{1,0:T(8,128)(2,1)}) custom-call(s32[2]{0:T(128)} %pad_add_fusion.place_ref, bf16[512,512]{1,0:T(8,128)(2,1)} %bitcast.14, bf16[512,512]{1,0:T(8,128)(2,1)} %bitcast.16, bf16[2048,512]{1,0:T(8,128)(2,1)} %bitcast.9, bf16[512,2048]{1,0:T(8,128)(2,1)} %in_ref.1, ...), custom_call_target="tpu_custom_call" | custom-call | tf_op jit(solution)/shard_map/layer/pallas_call | solution.py:495
  83.9 1.3 collective-permute-start
  85.2 26.1 %collective-permute-done.extra_ref = bf16[512,512]{1,0:T(8,128)(2,1)S(1)} collective-permute-done((bf16[512,512]{1,0:T(8,128)(2,1)}, bf16[512,512]{1,0:T(8,128)(2,1)S(1)}, u32[]{:S(2)}, u32[]{:S(2)}) %collective-permute-start) | collective-permute-done | bytes 524320 | tf_op jit(solution)/shard_map/ppermute | solution.py:575
  111.3 0.0 copy-start.1
  111.3 0.8 copy-done.1
  112.1 3.7 %finish.1 = bf16[512,512]{1,0:T(8,128)(2,1)} custom-call(s32[2]{0:T(128)} %pad_add_fusion.place_ref, bf16[512,512]{1,0:T(8,128)(2,1)} %bitcast.15, f32[512,512]{1,0:T(8,128)} %get-tuple-element.10.entry_ref, bf16[512,512]{1,0:T(8,128)(2,1)} %copy-done.1, bf16[512,512]{1,0:T(8,128)(2,1)} %bitcast.13), custom_call_target="tpu_custom_call" | custom-call | tf_op jit(solution)/shard_map/finish/pallas_call | solution.py:551
  115.8 25.3 %all_to_all.5 = bf16[16,32,512]{2,1,0:T(8,128)(2,1)} all-to-all(bf16[16,32,512]{2,1,0:T(8,128)(2,1)} %bitcast.10), channel_id=1, replica_groups=mesh['col'=16,'seq'=2] {'col'}, dimensions={0} | all-to-all | bytes 1048576 | tf_op jit(solution)/shard_map/all_to_all | solution.py:577
  141.2 0.0 all-gather.2.cloned.1.call-update
  141.2 0.1 subtract_clamp_fusion
  141.3 0.7 min.12.count_ref
  141.9 0.0 copy-done.2
  141.9 4.6 %all_gather.6 = s32[32,512]{1,0:T(8,128)S(1)} all-gather(s32[16,512]{1,0:T(8,128)S(1)} %copy-done.2), channel_id=1, replica_groups=mesh['col'=16,'seq'=2] {'seq'}, dimensions={0}, use_global_device_ids=true | all-gather | bytes 98304 | tf_op jit(solution)/shard_map/all_gather | solution.py:569
  146.5 0.8 fusion.5
  147.3 0.7 broadcast_in_dim.20.slot_ref
  148.0 13.1 %all-gather.2.cloned.1.call-done.grad_ref = bf16[32,32,512]{2,1,0:T(8,128)(2,1)} async-done(((bf16[16,32,512]{2,1,0:T(8,128)(2,1)}), bf16[32,32,512]{2,1,0:T(8,128)(2,1)}) %all-gather.2.cloned.1.call-update) | async-done | bytes 1048592 | tf_op jit(solution)/shard_map/all_gather | solution.py:584
  161.1 43.8 %scatter.1 = f32[32,32768]{1,0:T(8,128)} custom-call(s32[32,512]{1,0:T(8,128)} %get-tuple-element.13.rows_ref, s32[32]{0:T(128)} %min.12.count_ref, s32[32,1,512]{2,1,0:T(1,128)} %broadcast_in_dim.20.slot_ref, bf16[32,32,512]{2,1,0:T(8,128)(2,1)} %all-gather.2.cloned.1.call-done.grad_ref), custom_call_target="tpu_custom_call" | custom-call | tf_op jit(solution)/shard_map/scatter/pallas_call | solution.py:245
  (1 shorter events, 0.0 us)
Async XLA Ops:
  7.2 6.1 %copy-start = (bf16[512,512]{1,0:T(8,128)(2,1)S(1)}, bf16[512,512]{1,0:T(8,128)(2,1)}, u32[]{:S(2)}) copy-start(bf16[512,512]{1,0:T(8,128)(2,1)} %out_w_ref.1) | copy-start | bytes 1572868
  7.2 7.1 %copy-start.3 = (s32[16]{0:T(128)S(1)}, s32[16]{0:T(128)}, u32[]{:S(2)}) copy-start(s32[16]{0:T(128)} %param.7) | copy-start | bytes 196
  7.2 153.9 %all-gather.2.cloned.1.call-start = ((), (), s32[]{:S(2)}) async-start(), calls=%async_computation.1 | async-start | bytes 1572864 | tf_op jit(solution)/shard_map/all_gather | solution.py:584
  57.1 84.8 %copy-start.2 = (s32[16,512]{1,0:T(8,128)S(1)}, s32[16,512]{1,0:T(8,128)}, u32[]{:S(2)}) copy-start(s32[16,512]{1,0:T(8,128)} %param.6) | copy-start | bytes 98308
  83.9 27.4 %collective-permute-start = (bf16[512,512]{1,0:T(8,128)(2,1)}, bf16[512,512]{1,0:T(8,128)(2,1)S(1)}, u32[]{:S(2)}, u32[]{:S(2)}) collective-permute-start(bf16[512,512]{1,0:T(8,128)(2,1)} %get-tuple-element.11), channel_id=1, source_target_pairs={{1,0},{3,2},{5,4},{7,6},{9,8},{11,10},{13,12},{15,14},{17,16},{19,... | collective-permute-start | bytes 1572872 | tf_op jit(solution)/shard_map/ppermute | solution.py:575
  111.3 0.8 copy-start.1
Sparse Core Ops, SparseCore 0:
  141.3 19.7 all-gather.1

commit v2 on v1

--- a/solution.py
+++ b/solution.py
@@ -27,8 +27,8 @@
 
 
 def lookup_kernel(
-    rows_ref, slot_ref, table_ref, own_ref, peer_ref,
-    packed, picked, slab, own, peer, own_sent, own_got, peer_sent, peer_got,
+    rows_ref, slot_ref, table_ref, items_ref, own_ref, peer_ref, twin_items_ref,
+    packed, picked, slab, own, peer, twin, own_sent, own_got, peer_sent, peer_got, twin_sems,
 ):
     feat, table_cols = table_ref.shape
     users, _, seq_rows = slot_ref.shape
@@ -39,16 +39,7 @@
     barrier = pltpu.get_barrier_semaphore()
     halves = lax.axis_size("seq")
 
-    def greet(other, carry):
-        @pl.when(other != col * halves + seq)
-        def _():
-            pl.semaphore_signal(
-                barrier, inc=1, device_id=(other // halves, other % halves), device_id_type=MESH
-            )
-
-        return carry
-
-    lax.fori_loop(0, users * halves, greet, 0)
+    greet_all(barrier, users, halves, col * halves + seq)
 
     def pack(block, carry):
         base = pl.multiple_of(block * span, span)
@@ -59,6 +50,15 @@
 
     lax.fori_loop(0, table_cols // span, pack, 0, unroll=2)
     pl.semaphore_wait(barrier, users * halves - 1)
+    items_copy = pltpu.make_async_remote_copy(
+        src_ref=items_ref,
+        dst_ref=twin,
+        send_sem=twin_sems.at[0],
+        recv_sem=twin_sems.at[1],
+        device_id=(col, 1 - seq),
+        device_id_type=MESH,
+    )
+    items_copy.start()
 
     def to_own(user, sender):
         return pltpu.make_async_remote_copy(
@@ -111,6 +111,8 @@
 
     lax.fori_loop(0, users, one_user, 0)
     own_ref[col] = slab[col]
+    items_copy.wait()
+    twin_items_ref[...] = twin[...]
 
     def collect(step, carry):
         other = lax.rem(col + 1 + step, users)
@@ -157,22 +159,25 @@
     slabs = (users, feat, seq_rows)
     return pl.pallas_call(
         lookup_kernel,
-        out_shape=(jax.ShapeDtypeStruct(slabs, jnp.bfloat16),) * 2,
-        in_specs=[pl.BlockSpec(memory_space=pltpu.SMEM), vmem, vmem],
-        out_specs=(vmem, vmem),
+        out_shape=(jax.ShapeDtypeStruct(slabs, jnp.bfloat16),) * 2
+        + (jax.ShapeDtypeStruct(items.shape, items.dtype),),
+        in_specs=[pl.BlockSpec(memory_space=pltpu.SMEM), vmem, vmem, vmem],
+        out_specs=(vmem,) * 3,
         scratch_shapes=[
             pltpu.VMEM((table_cols * feat // LANES, LANES), jnp.float32),
             pltpu.VMEM((seq_rows, LANES), jnp.float32),
             pltpu.VMEM(slabs, jnp.bfloat16),
             pltpu.VMEM(slabs, jnp.bfloat16),
             pltpu.VMEM(slabs, jnp.bfloat16),
+            pltpu.VMEM(items.shape, items.dtype),
         ]
-        + [pltpu.SemaphoreType.DMA((users,))] * 4,
+        + [pltpu.SemaphoreType.DMA((users,))] * 4
+        + [pltpu.SemaphoreType.DMA((2,))],
         compiler_params=pltpu.CompilerParams(
             vmem_limit_bytes=VMEM_BYTES, collective_id=0, has_side_effects=True
         ),
         name="lookup",
-    )(row, slot[:, None], item_table)
+    )(row, slot[:, None], item_table, items)
 
 
 def scatter_kernel(rows_ref, count_ref, slot_ref, grad_ref, out_ref, placed, *sums):
@@ -293,14 +298,14 @@
 
 
 def layer_kernel(
-    place_ref, own_ref, peer_ref, in_turned_ref, in_ref, out_turned_ref, out_w_ref, cot_ref,
+    lengths_ref, own_ref, peer_ref, in_turned_ref, in_ref, out_turned_ref, out_w_ref, cot_ref,
     out_ref, entry_ref, partial_ref,
     normed, act, slope, act_peer, slope_peer, query_rows, att, scale, gated, grad_cols, grad_rows,
     point, bend, point_peer, bend_peer, pre_grad, pre_grad_peer, query_grad,
 ):
     hidden, rows = own_ref.shape
-    seq_index = place_ref[0]
-    length = place_ref[1]
+    seq_index = lax.axis_index("seq")
+    length = lengths_ref[lax.axis_index("col")]
     first = seq_index * rows
     score_scale = DH ** (-0.5)
     length_scale = 1.0 / LEN
@@ -489,7 +494,7 @@
         partial_ref[...] = jnp.zeros_like(partial_ref)
 
 
-def layer(place, own, peer, input_weight, output_weight, cot):
+def layer(lengths, own, peer, input_weight, output_weight, cot):
     hidden, rows = own.shape
     vmem = pl.BlockSpec(memory_space=pltpu.VMEM)
     return pl.pallas_call(
@@ -523,66 +528,164 @@
         ],
         compiler_params=pltpu.CompilerParams(vmem_limit_bytes=VMEM_BYTES),
         name="layer",
-    )(place, own, peer, input_weight.T, input_weight, output_weight.T, output_weight, cot)
-
-
-def finish_kernel(place_ref, own_ref, entry_ref, extra_ref, cot_ref, out_ref):
+    )(lengths, own, peer, input_weight.T, input_weight, output_weight.T, output_weight, cot)
+
+
+def greet_all(barrier, users, halves, me):
+    def greet(other, carry):
+        @pl.when(other != me)
+        def _():
+            pl.semaphore_signal(
+                barrier, inc=1, device_id=(other // halves, other % halves), device_id_type=MESH
+            )
+
+        return carry
+
+    lax.fori_loop(0, users * halves, greet, 0)
+
+
+def back_kernel(
+    lengths_ref, own_ref, entry_ref, partial_ref, cot_ref, out_ref,
+    extra, grad, mine, others, extra_sems, sent, got, passed, passed_got,
+):
     hidden, rows = own_ref.shape
-    first = place_ref[0] * rows
-    length = place_ref[1]
+    users, feat, _ = grad.shape
+    halves = lax.axis_size("seq")
+    col = lax.axis_index("col")
+    seq = lax.axis_index("seq")
+    length = lengths_ref[col]
+    first = seq * rows
+    barrier = pltpu.get_barrier_semaphore()
+    greet_all(barrier, users, halves, col * halves + seq)
+    pl.semaphore_wait(barrier, users * halves - 1)
+
+    extra_copy = pltpu.make_async_remote_copy(
+        src_ref=partial_ref,
+        dst_ref=extra,
+        send_sem=extra_sems.at[0],
+        recv_sem=extra_sems.at[1],
+        device_id=(col, 0),
+        device_id_type=MESH,
+    )
+
+    @pl.when(seq == 1)
+    def _():
+        extra_copy.start()
 
     def chunk(step, carry):
         at = pl.ds(pl.multiple_of(step * LANES, LANES), LANES)
         centered, inverse = column_stats(own_ref[:, at].astype(F32))
-        grad = entry_ref[:, at] + extra_ref[:, at].astype(F32)
-        back = norm_back(centered * inverse, inverse, grad)
+        received = jnp.where(seq == 0, extra[:, at].astype(F32), 0.0)
+        back = norm_back(centered * inverse, inverse, entry_ref[:, at] + received)
         lane_valid = (
             lax.broadcasted_iota(jnp.int32, (1, LANES), 1) + first + step * LANES < length
         )
-        cot = jnp.where(lane_valid, turn(cot_ref[at, :]), 0.0)
-        out_ref[:, at] = (cot + back).astype(BF16)
-        return carry
+        total = jnp.where(lane_valid, turn(cot_ref[at, :]), 0.0) + back
+        grad[:, :, at] = total.reshape(users, feat, LANES).astype(BF16)
+        return carry
+
+    @pl.when(seq == 1)
+    def _():
+        extra[...] = jnp.zeros_like(extra)
+
+    @pl.when(seq == 0)
+    def _():
+        extra_copy.wait_recv()
 
     lax.fori_loop(0, rows // LANES, chunk, 0)
 
-
-def finish(place, own, entry, extra, cot):
+    def to_owner(user, sender):
+        return pltpu.make_async_remote_copy(
+            src_ref=grad.at[user],
+            dst_ref=mine.at[sender],
+            send_sem=sent.at[user],
+            recv_sem=got.at[sender],
+            device_id=(user, seq),
+            device_id_type=MESH,
+        )
+
+    def to_twin(source, sender):
+        return pltpu.make_async_remote_copy(
+            src_ref=source.at[sender],
+            dst_ref=others.at[sender],
+            send_sem=passed.at[sender],
+            recv_sem=passed_got.at[sender],
+            device_id=(col, 1 - seq),
+            device_id_type=MESH,
+        )
+
+    def send(step, carry):
+        user = lax.rem(col + 1 + step, users)
+        to_owner(user, col).start()
+        return carry
+
+    lax.fori_loop(0, users - 1, send, 0)
+    to_twin(grad, col).start()
+    out_ref[col] = grad[col]
+
+    def forward(step, carry):
+        sender = lax.rem(col + users - 1 - step, users)
+        to_owner(sender, sender).wait_recv()
+        to_twin(mine, sender).start()
+        out_ref[sender] = mine[sender]
+        return carry
+
+    lax.fori_loop(0, users - 1, forward, 0)
+
+    def collect(step, carry):
+        sender = lax.rem(col + users - step, users)
+        to_twin(mine, sender).wait_recv()
+        out_ref[users + sender] = others[sender]
+        return carry
+
+    lax.fori_loop(0, users, collect, 0)
+
+    def leave(step, carry):
+        user = lax.rem(col + 1 + step, users)
+        to_owner(user, col).wait_send()
+        to_twin(mine, user).wait_send()
+        return carry
+
+    lax.fori_loop(0, users - 1, leave, 0)
+    to_twin(grad, col).wait_send()
+
+    @pl.when(seq == 1)
+    def _():
+        extra_copy.wait_send()
+
+
+def send_back(lengths, own, entry, partial, cot, users):
+    hidden, rows = own.shape
     vmem = pl.BlockSpec(memory_space=pltpu.VMEM)
+    slabs = (users, hidden // users, rows)
     return pl.pallas_call(
-        finish_kernel,
-        out_shape=jax.ShapeDtypeStruct(own.shape, BF16),
+        back_kernel,
+        out_shape=jax.ShapeDtypeStruct((2 * users,) + slabs[1:], BF16),
         in_specs=[pl.BlockSpec(memory_space=pltpu.SMEM)] + [vmem] * 4,
         out_specs=vmem,
-        compiler_params=pltpu.CompilerParams(vmem_limit_bytes=VMEM_BYTES),
-        name="finish",
-    )(place, own, entry, extra, cot)
+        scratch_shapes=[pltpu.VMEM((hidden, rows), BF16)]
+        + [pltpu.VMEM(slabs, BF16)] * 3
+        + [pltpu.SemaphoreType.DMA((2,))]
+        + [pltpu.SemaphoreType.DMA((users,))] * 4,
+        compiler_params=pltpu.CompilerParams(
+            vmem_limit_bytes=VMEM_BYTES, collective_id=1, has_side_effects=True
+        ),
+        name="send_back",
+    )(lengths, own, entry, partial, cot)
 
 
 def per_device(history_items, lengths, item_table, input_weight, output_weight, output_cotangent):
     user_count, seq_rows = history_items.shape
     feat_cols = item_table.shape[0]
-    col_index = lax.axis_index("col")
     seq_index = lax.axis_index("seq")
-    chosen = jnp.arange(lengths.shape[0], dtype=jnp.int32) == col_index
-    length = jnp.sum(jnp.where(chosen, lengths, 0))
-    place = jnp.stack([seq_index, length]).astype(jnp.int32)
-    every_item = lax.all_gather(history_items, "seq", axis=0, tiled=True)
-    own, peer = lookup(history_items, item_table)
+    own, peer, twin_items = lookup(history_items, item_table)
     own = own.reshape(user_count * feat_cols, seq_rows)
     peer = peer.reshape(user_count * feat_cols, seq_rows)
     cot = output_cotangent[0]
-    layer_output, entry, partial = layer(place, own, peer, input_weight, output_weight, cot)
-    extra = lax.ppermute(partial, "seq", [(1, 0)])
-    input_grad = finish(place, own, entry, extra, cot)
-    back = lax.all_to_all(
-        input_grad.reshape(user_count, feat_cols, seq_rows),
-        "col",
-        split_axis=0,
-        concat_axis=0,
-        tiled=True,
-    )
-    every_grad = lax.all_gather(back, "seq", axis=0, tiled=True)
-    starts = seq_rows * jnp.arange(lax.axis_size("seq"), dtype=jnp.int32)
+    layer_output, entry, partial = layer(lengths, own, peer, input_weight, output_weight, cot)
+    every_grad = send_back(lengths, own, entry, partial, cot, user_count)
+    every_item = jnp.concatenate([history_items, twin_items], axis=0)
+    starts = seq_rows * jnp.stack([seq_index, 1 - seq_index])
     counts = jnp.clip(lengths[None, :] - starts[:, None], 0, seq_rows).reshape(-1)
     owned_rows = item_table.shape[1] // lax.axis_size("seq")
     table_gradient = scatter(every_item, counts, every_grad, owned_rows, seq_index)

time: 215 us -> 178 us (0.83); the launches traced: 212 us -> 179 us
  Pallas kernels: 115 us -> 170 us
  waiting for transfers between devices: 39.3 us -> 0 us
  blocking collectives: 29.9 us -> 0 us
  between operations: 14.1 us -> 0.68 us
  local copies, waits for them, and re-layouts: 7.69 us -> 4.82 us
    pallas_call x1, Pallas kernels: 3.75 us -> 56.6 us  [send_back(): pl.pallas_call(back_kernel, out_shape=jax.ShapeDtypeStruct((2 * users,) +...]
    ppermute x1 -> x0, waiting for transfers between devices: 26.1 us -> none  [per_device(): extra = lax.ppermute(partial, 'seq', [(1, 0)])]
    all_to_all x1 -> x0, blocking collectives: 25.3 us -> none  [per_device(): lax.all_to_all(input_grad.reshape(user_count, feat_cols, seq_rows), 'col'...]
    all_gather x1 -> x0, waiting for transfers between devices: 13.1 us -> none  [per_device(): every_grad = lax.all_gather(back, 'seq', axis=0, tiled=True)]
    all_gather x1 -> x0, blocking collectives: 4.58 us -> none  [per_device(): every_item = lax.all_gather(history_items, 'seq', axis=0, tiled=True)]
    unnamed x10 -> x13, local copies, waits for them, and re-layouts: 5.72 us -> 3.56 us
  transfers between devices with their start and end apart: 2 -> 0, of which waited for: 2 -> 0; matrix products, arithmetic and copies ran while one was open for 1% -> 0% of each run, Pallas kernels for 0% -> 0%
where the time goes in v2:
time: 178 us; the launch traced here: 179 us
  Pallas kernels  170 us (96%)
  local copies, waits for them, and re-layouts  4.82 us (3%)
  other arithmetic  3.85 us (2%)
    pallas_call x1, Pallas kernels, send_back(): pl.pallas_call(back_kernel, out_shape=jax.ShapeDtypeStruct((2 * users,) +...  56.6 us
    pallas_call x1, Pallas kernels, scatter(): pl.pallas_call(scatter_kernel, out_shape=jax.ShapeDtypeStruct((feat, owne...  45.3 us
    pallas_call x1, Pallas kernels, lookup(): pl.pallas_call(lookup_kernel, out_shape=(jax.ShapeDtypeStruct(slabs, jnp....  41.1 us
    pallas_call x1, Pallas kernels, layer(): pl.pallas_call(layer_kernel, out_shape=(jax.ShapeDtypeStruct((rows, hidde...  26.8 us

profile of v2, /device:TPU:0, one launch (start us, length us, event | category | flops | bytes accessed | tf_op | source)
XLA Modules:
  0.0 179.1 jit_solution(15871863198858233055)
XLA Ops:
  0.6 1.4 constant_dynamic-update-slice_fusion.1
  2.1 0.6 broadcast_in_dim.6.slot_ref
  2.7 0.0 copy-start
  2.7 41.1 %lookup.1 = (bf16[16,32,512]{2,1,0:T(8,128)(2,1)}, bf16[16,32,512]{2,1,0:T(8,128)(2,1)}, s32[16,512]{1,0:T(8,128)}) custom-call(s32[16,512]{1,0:T(8,128)} %get-tuple-element.15.rows_ref, s32[16,1,512]{2,1,0:T(1,128)} %broadcast_in_dim.6.slot_ref, f32[32,65536]{1,0:T(8,128)} %table_ref.1, s32[16,512]{1,0:T(8,128)} %items_ref.1), custom_call_target="tpu_custom_call" | custom-call | tf_op jit(solution)/shard_map/lookup/pallas_call | solution.py:160
  43.8 0.0 copy-start.1
  43.8 0.0 copy-done
  43.8 2.5 %copy.8 = bf16[512,2048]{0,1:T(8,128)(2,1)} copy(bf16[512,2048]{1,0:T(8,128)(2,1)S(1)} %copy-done) | data formatting | bytes 4194304 | tf_op args[3]
  46.3 0.0 copy-start.3
  46.3 0.0 copy-start.4
  46.3 0.0 copy-start.2
  46.3 0.0 copy-done.1
  46.3 1.0 copy.9
  47.3 26.8 %layer.1 = (bf16[512,512]{1,0:T(8,128)(2,1)}, f32[512,512]{1,0:T(8,128)}, bf16[512,512]{1,0:T(8,128)(2,1)}) custom-call(s32[16]{0:T(128)} %lengths_ref.3, bf16[512,512]{1,0:T(8,128)(2,1)} %bitcast.12, bf16[512,512]{1,0:T(8,128)(2,1)} %bitcast.14, bf16[2048,512]{1,0:T(8,128)(2,1)} %bitcast.8, bf16[512,2048]{1,0:T(8,128)(2,1)} %in_ref.1, ...), custom_call_target="tpu_custom_call" | custom-call | tf_op jit(solution)/shard_map/layer/pallas_call | solution.py:500
  74.1 0.0 copy-done.3
  74.1 0.7 fusion.3.rows_ref
  74.8 0.1 add_multiply_fusion
  74.9 0.0 copy-done.4
  74.9 0.1 subtract_clamp_fusion
  75.0 0.6 min.12.count_ref
  75.6 0.0 copy-done.2
  75.7 1.6 compare_select_fusion.2.slot_ref
  77.2 56.6 %send_back.1.grad_ref = bf16[32,32,512]{2,1,0:T(8,128)(2,1)} custom-call(s32[16]{0:T(128)} %lengths_ref.3, bf16[512,512]{1,0:T(8,128)(2,1)} %bitcast.13, f32[512,512]{1,0:T(8,128)} %get-tuple-element.12.entry_ref, bf16[512,512]{1,0:T(8,128)(2,1)} %get-tuple-element.13.partial_ref, bf16[512,512]{1,0:T(8,128)(2,1)} %bitcast.11), custom_call_target="tpu_custom_call" | custom-call | tf_op jit(solution)/shard_map/send_back/pallas_call | solution.py:661
  133.8 45.3 %scatter.1 = f32[32,32768]{1,0:T(8,128)} custom-call(s32[32,512]{1,0:T(8,128)} %fusion.3.rows_ref, s32[32]{0:T(128)} %min.12.count_ref, s32[32,1,512]{2,1,0:T(1,128)} %compare_select_fusion.2.slot_ref, bf16[32,32,512]{2,1,0:T(8,128)(2,1)} %send_back.1.grad_ref), custom_call_target="tpu_custom_call" | custom-call | tf_op jit(solution)/shard_map/scatter/pallas_call | solution.py:250
  (3 shorter events, 0.1 us)
Async XLA Ops:
  2.7 41.1 %copy-start = (bf16[512,2048]{1,0:T(8,128)(2,1)S(1)}, bf16[512,2048]{1,0:T(8,128)(2,1)}, u32[]{:S(2)}) copy-start(bf16[512,2048]{1,0:T(8,128)(2,1)} %in_ref.1) | copy-start | bytes 6291460
  43.8 2.5 %copy-start.1 = (bf16[512,512]{1,0:T(8,128)(2,1)S(1)}, bf16[512,512]{1,0:T(8,128)(2,1)}, u32[]{:S(2)}) copy-start(bf16[512,512]{1,0:T(8,128)(2,1)} %out_w_ref.1) | copy-start | bytes 1572868
  46.3 27.8 %copy-start.3 = (s32[16,512]{1,0:T(8,128)S(1)}, s32[16,512]{1,0:T(8,128)}, u32[]{:S(2)}) copy-start(s32[16,512]{1,0:T(8,128)} %get-tuple-element.11) | copy-start | bytes 98308
  46.3 28.6 %copy-start.4 = (s32[16]{0:T(128)S(1)}, s32[16]{0:T(128)}, u32[]{:S(2)}) copy-start(s32[16]{0:T(128)} %lengths_ref.3) | copy-start | bytes 196
  46.3 29.3 %copy-start.2 = (s32[16,512]{1,0:T(8,128)S(1)}, s32[16,512]{1,0:T(8,128)}, u32[]{:S(2)}) copy-start(s32[16,512]{1,0:T(8,128)} %items_ref.1) | copy-start | bytes 98308

commit v3 on v2

--- a/solution.py
+++ b/solution.py
@@ -14,6 +14,9 @@
 
 
 LANES = 128
+BLOCK = 256
+F32 = jnp.float32
+BF16 = jnp.bfloat16
 MESH = pl.DeviceIdType.MESH
 COPIES = 8
 VMEM_BYTES = 58 * 1024 * 1024
@@ -24,6 +27,19 @@
     row = (items // (LANES * groups)) * LANES + items % LANES
     slot = (items // LANES) % groups
     return row, slot
+
+
+def greet_all(barrier, users, halves, me):
+    def greet(other, carry):
+        @pl.when(other != me)
+        def _():
+            pl.semaphore_signal(
+                barrier, inc=1, device_id=(other // halves, other % halves), device_id_type=MESH
+            )
+
+        return carry
+
+    lax.fori_loop(0, users * halves, greet, 0)
 
 
 def lookup_kernel(
@@ -44,11 +60,11 @@
     def pack(block, carry):
         base = pl.multiple_of(block * span, span)
         parts = [table_ref[:, pl.ds(base + g * LANES, LANES)] for g in range(groups)]
-        turned = jnp.concatenate(parts, axis=0).T
+        turned = jnp.concatenate(parts, axis=0).astype(BF16).T.astype(F32)
         packed[pl.ds(pl.multiple_of(block * LANES, LANES), LANES), :] = turned
         return carry
 
-    lax.fori_loop(0, table_cols // span, pack, 0, unroll=2)
+    lax.fori_loop(0, table_cols // span, pack, 0, unroll=4)
     pl.semaphore_wait(barrier, users * halves - 1)
     items_copy = pltpu.make_async_remote_copy(
         src_ref=items_ref,
@@ -92,7 +108,7 @@
 
         lax.fori_loop(0, seq_rows // 32, pick, 0)
         for part in range(seq_rows // LANES):
-            turned = picked[pl.ds(part * LANES, LANES), :].T
+            turned = picked[pl.ds(part * LANES, LANES), :].astype(BF16).T.astype(F32)
             slot = slot_ref[user, :, pl.ds(part * LANES, LANES)]
             total = jnp.zeros((feat, LANES), jnp.float32)
             for g in range(groups):
@@ -204,7 +220,7 @@
             spread = jnp.concatenate(
                 [jnp.where(slot == g, grad, 0.0) for g in range(groups)], axis=0
             )
-            placed[at, :] = spread.T
+            placed[at, :] = spread.astype(BF16).T.astype(F32)
             return inner
 
         lax.fori_loop(0, (count + LANES - 1) // LANES, place, 0)
@@ -238,7 +254,7 @@
             out_ref[:, pl.ds(base + g * LANES, LANES)] = turned[g * feat : (g + 1) * feat, :]
         return carry
 
-    lax.fori_loop(0, owned // span, unpack, 0, unroll=2)
+    lax.fori_loop(0, owned // span, unpack, 0, unroll=4)
 
 
 def scatter(items, counts, grads, owned, seq_index):
@@ -264,11 +280,6 @@
     )(row, counts, slot[:, None], grads)
 
 
-BLOCK = 256
-F32 = jnp.float32
-BF16 = jnp.bfloat16
-
-
 def dot(left, right):
     return jnp.dot(left, right, preferred_element_type=F32)
 
@@ -299,20 +310,26 @@
 
 def layer_kernel(
     lengths_ref, own_ref, peer_ref, in_turned_ref, in_ref, out_turned_ref, out_w_ref, cot_ref,
-    out_ref, entry_ref, partial_ref,
+    out_ref, back_ref,
     normed, act, slope, act_peer, slope_peer, query_rows, att, scale, gated, grad_cols, grad_rows,
     point, bend, point_peer, bend_peer, pre_grad, pre_grad_peer, query_grad,
+    entry, partial, extra, grad, mine, others, extra_sems, sent, got, passed, passed_got,
 ):
     hidden, rows = own_ref.shape
-    seq_index = lax.axis_index("seq")
-    length = lengths_ref[lax.axis_index("col")]
-    first = seq_index * rows
+    users, feat, _ = grad.shape
+    halves = lax.axis_size("seq")
+    col = lax.axis_index("col")
+    seq = lax.axis_index("seq")
+    length = lengths_ref[col]
+    first = seq * rows
+    barrier = pltpu.get_barrier_semaphore()
+    greet_all(barrier, users, halves, col * halves + seq)
     score_scale = DH ** (-0.5)
     length_scale = 1.0 / LEN
     lane_pos = lax.broadcasted_iota(jnp.int32, (1, rows), 1)
     valid = lane_pos + first < length
     valid_peer = lane_pos < length
-    has_peer = seq_index == 1
+    has_peer = seq == 1
 
     def normalize(ref):
         def chunk(step, carry):
@@ -424,88 +441,184 @@
 
     lax.fori_loop(0, rows // LANES, mix, 0)
 
+    def backward_peer(head, carry):
+        grad_rows[head] = turn(grad_cols[head_rows(0, head), :]).astype(BF16)
+        value_total = jnp.zeros((DH, rows), F32)
+        key_total = jnp.zeros((DH, rows), F32)
+        for i in range(blocks):
+            at_i = pl.ds(i * BLOCK, BLOCK)
+            weight_grad = dot(grad_rows[head, at_i, :], act_peer[head_rows(0, head), :])
+            score_grad = (weight_grad * bend_peer[head, at_i, :].astype(F32)).astype(BF16)
+            value_total += dot(grad_cols[head_rows(0, head), at_i], point_peer[head, at_i, :])
+            key_total += dot(act[head_rows(2 * hidden, head), at_i], score_grad)
+            query_grad[head_rows(0, head), at_i] = dot_last(
+                act_peer[head_rows(hidden, head), :], score_grad
+            )
+        value_total = jnp.where(valid_peer, value_total, 0.0)
+        pre_grad_peer[head_rows(0, head), :] = (
+            value_total * slope_peer[head_rows(0, head), :]
+        ).astype(BF16)
+        pre_grad_peer[head_rows(hidden, head), :] = (
+            key_total * score_scale * slope_peer[head_rows(hidden, head), :]
+        ).astype(BF16)
+        return carry
+
+    def leave_peer(step, carry):
+        at = pl.ds(pl.multiple_of(step * BLOCK, BLOCK), BLOCK)
+        total = dot(in_ref[at, hidden : 2 * hidden], pre_grad_peer[0:hidden, :])
+        total += dot(in_ref[at, 3 * hidden :], pre_grad_peer[hidden:, :])
+        partial[at, :] = total.astype(BF16)
+        return carry
+
+    pl.semaphore_wait(barrier, users * halves - 1)
+    extra_copy = pltpu.make_async_remote_copy(
+        src_ref=partial,
+        dst_ref=extra,
+        send_sem=extra_sems.at[0],
+        recv_sem=extra_sems.at[1],
+        device_id=(col, 0),
+        device_id_type=MESH,
+    )
+
+    @pl.when(has_peer)
+    def _():
+        lax.fori_loop(0, H, backward_peer, 0)
+        lax.fori_loop(0, hidden // BLOCK, leave_peer, 0)
+        extra_copy.start()
+        extra[...] = jnp.zeros_like(extra)
+
+    @pl.when(jnp.logical_not(has_peer))
+    def _():
+        def rows_only(head, carry):
+            grad_rows[head] = turn(grad_cols[head_rows(0, head), :]).astype(BF16)
+            return carry
+
+        lax.fori_loop(0, H, rows_only, 0)
+        query_grad[...] = jnp.zeros_like(query_grad)
+
     def backward(head, carry):
-        grad_rows[...] = turn(grad_cols[head_rows(0, head), :]).astype(BF16)
-        query_grad[...] = jnp.zeros_like(query_grad)
-
-        @pl.when(has_peer)
-        def _():
-            value_total = jnp.zeros((DH, rows), F32)
-            key_total = jnp.zeros((DH, rows), F32)
-            for i in range(blocks):
-                at_i = pl.ds(i * BLOCK, BLOCK)
-                weight_grad = dot(grad_rows[at_i, :], act_peer[head_rows(0, head), :])
-                score_grad = (weight_grad * bend_peer[head, at_i, :].astype(F32)).astype(BF16)
-                value_total += dot(grad_cols[head_rows(0, head), at_i], point_peer[head, at_i, :])
-                key_total += dot(act[head_rows(2 * hidden, head), at_i], score_grad)
-                query_grad[:, at_i] = dot_last(act_peer[head_rows(hidden, head), :], score_grad)
-            value_total = jnp.where(valid_peer, value_total, 0.0)
-            pre_grad_peer[head_rows(0, head), :] = (
-                value_total * slope_peer[head_rows(0, head), :]
-            ).astype(BF16)
-            pre_grad_peer[head_rows(hidden, head), :] = (
-                key_total * score_scale * slope_peer[head_rows(hidden, head), :]
-            ).astype(BF16)
-
         value_parts = [jnp.zeros((DH, BLOCK), F32) for _ in range(blocks)]
         key_parts = [jnp.zeros((DH, BLOCK), F32) for _ in range(blocks)]
         for i in range(blocks):
             at_i = pl.ds(i * BLOCK, BLOCK)
+            query_total = query_grad[head_rows(0, head), at_i]
             for j in range(i + 1):
                 at_j = pl.ds(j * BLOCK, BLOCK)
-                weight_grad = dot(grad_rows[at_i, :], act[head_rows(hidden, head), at_j])
+                weight_grad = dot(grad_rows[head, at_i, :], act[head_rows(hidden, head), at_j])
                 score_grad = (weight_grad * bend[head, at_i, at_j].astype(F32)).astype(BF16)
                 value_parts[j] += dot(grad_cols[head_rows(0, head), at_i], point[head, at_i, at_j])
                 key_parts[j] += dot(act[head_rows(2 * hidden, head), at_i], score_grad)
-                query_grad[:, at_i] += dot_last(act[head_rows(3 * hidden, head), at_j], score_grad)
+                query_total += dot_last(act[head_rows(3 * hidden, head), at_j], score_grad)
+            query_at = head_rows(2 * hidden, head)
+            pre_grad[query_at, at_i] = (query_total * score_scale * slope[query_at, at_i]).astype(
+                BF16
+            )
         value_total = jnp.where(valid, jnp.concatenate(value_parts, axis=1), 0.0)
         key_total = jnp.concatenate(key_parts, axis=1) * score_scale
-        for start, total in (
-            (hidden, value_total),
-            (2 * hidden, query_grad[...] * score_scale),
-            (3 * hidden, key_total),
-        ):
+        for start, total in ((hidden, value_total), (3 * hidden, key_total)):
             at = head_rows(start, head)
             pre_grad[at, :] = (total * slope[at, :]).astype(BF16)
         return carry
 
     lax.fori_loop(0, H, backward, 0)
 
+    def leave_own(step, carry):
+        at = pl.ds(pl.multiple_of(step * BLOCK, BLOCK), BLOCK)
+        entry[at, :] = dot(in_ref[at, :], pre_grad[...])
+        return carry
+
+    lax.fori_loop(0, hidden // BLOCK, leave_own, 0)
+
+    @pl.when(seq == 0)
+    def _():
+        extra_copy.wait_recv()
+
+    def chunk(step, carry):
+        at = pl.ds(pl.multiple_of(step * LANES, LANES), LANES)
+        centered, inverse = column_stats(own_ref[:, at].astype(F32))
+        received = jnp.where(seq == 0, extra[:, at].astype(F32), 0.0)
+        back = norm_back(centered * inverse, inverse, entry[:, at] + received)
+        lane_valid = (
+            lax.broadcasted_iota(jnp.int32, (1, LANES), 1) + first + step * LANES < length
+        )
+        total = jnp.where(lane_valid, turn(cot_ref[at, :]), 0.0) + back
+        grad[:, :, at] = total.reshape(users, feat, LANES).astype(BF16)
+        return carry
+
+    lax.fori_loop(0, rows // LANES, chunk, 0)
+
+    def to_owner(user, sender):
+        return pltpu.make_async_remote_copy(
+            src_ref=grad.at[user],
+            dst_ref=mine.at[sender],
+            send_sem=sent.at[user],
+            recv_sem=got.at[sender],
+            device_id=(user, seq),
+            device_id_type=MESH,
+        )
+
+    def to_twin(source, sender):
+        return pltpu.make_async_remote_copy(
+            src_ref=source.at[sender],
+            dst_ref=others.at[sender],
+            send_sem=passed.at[sender],
+            recv_sem=passed_got.at[sender],
+            device_id=(col, 1 - seq),
+            device_id_type=MESH,
+        )
+
+    def send(step, carry):
+        user = lax.rem(col + 1 + step, users)
+        to_owner(user, col).start()
+        return carry
+
+    lax.fori_loop(0, users - 1, send, 0)
+    to_twin(grad, col).start()
+    back_ref[col] = grad[col]
+
+    def forward(step, carry):
+        sender = lax.rem(col + users - 1 - step, users)
+        to_owner(sender, sender).wait_recv()
+        to_twin(mine, sender).start()
+        back_ref[sender] = mine[sender]
+        return carry
+
+    lax.fori_loop(0, users - 1, forward, 0)
+
+    def collect(step, carry):
+        sender = lax.rem(col + users - step, users)
+        to_twin(mine, sender).wait_recv()
+        back_ref[users + sender] = others[sender]
+        return carry
+
+    lax.fori_loop(0, users, collect, 0)
+
     def leave(step, carry):
-        at = pl.ds(pl.multiple_of(step * BLOCK, BLOCK), BLOCK)
-        entry_ref[at, :] = dot(in_ref[at, :], pre_grad[...])
-        return carry
-
-    lax.fori_loop(0, hidden // BLOCK, leave, 0)
-
-    @pl.when(has_peer)
-    def _():
-        def leave_peer(step, carry):
-            at = pl.ds(pl.multiple_of(step * BLOCK, BLOCK), BLOCK)
-            total = dot(in_ref[at, hidden : 2 * hidden], pre_grad_peer[0:hidden, :])
-            total += dot(in_ref[at, 3 * hidden :], pre_grad_peer[hidden:, :])
-            partial_ref[at, :] = total.astype(BF16)
-            return carry
-
-        lax.fori_loop(0, hidden // BLOCK, leave_peer, 0)
-
-    @pl.when(jnp.logical_not(has_peer))
-    def _():
-        partial_ref[...] = jnp.zeros_like(partial_ref)
-
-
-def layer(lengths, own, peer, input_weight, output_weight, cot):
+        user = lax.rem(col + 1 + step, users)
+        to_owner(user, col).wait_send()
+        to_twin(mine, user).wait_send()
+        return carry
+
+    lax.fori_loop(0, users - 1, leave, 0)
+    to_twin(grad, col).wait_send()
+
+    @pl.when(seq == 1)
+    def _():
+        extra_copy.wait_send()
+
+
+def layer(lengths, own, peer, input_weight, output_weight, cot, users):
     hidden, rows = own.shape
+    slabs = (users, hidden // users, rows)
     vmem = pl.BlockSpec(memory_space=pltpu.VMEM)
     return pl.pallas_call(
         layer_kernel,
         out_shape=(
             jax.ShapeDtypeStruct((rows, hidden), BF16),
-            jax.ShapeDtypeStruct((hidden, rows), F32),
-            jax.ShapeDtypeStruct((hidden, rows), BF16),
+            jax.ShapeDtypeStruct((2 * users,) + slabs[1:], BF16),
         ),
         in_specs=[pl.BlockSpec(memory_space=pltpu.SMEM)] + [vmem] * 7,
-        out_specs=(vmem,) * 3,
+        out_specs=(vmem,) * 2,
         scratch_shapes=[
             pltpu.VMEM((hidden, rows), BF16),
             pltpu.VMEM((4 * hidden, rows), BF16),
@@ -517,161 +630,26 @@
             pltpu.VMEM((1, rows), F32),
             pltpu.VMEM((hidden, rows), BF16),
             pltpu.VMEM((hidden, rows), BF16),
-            pltpu.VMEM((rows, DH), BF16),
+            pltpu.VMEM((H, rows, DH), BF16),
             pltpu.VMEM((H, rows, rows), BF16),
             pltpu.VMEM((H, rows, rows), BF16),
             pltpu.VMEM((H, rows, rows), BF16),
             pltpu.VMEM((H, rows, rows), BF16),
             pltpu.VMEM((4 * hidden, rows), BF16),
             pltpu.VMEM((2 * hidden, rows), BF16),
-            pltpu.VMEM((DH, rows), F32),
-        ],
-        compiler_params=pltpu.CompilerParams(vmem_limit_bytes=VMEM_BYTES),
-        name="layer",
-    )(lengths, own, peer, input_weight.T, input_weight, output_weight.T, output_weight, cot)
-
-
-def greet_all(barrier, users, halves, me):
-    def greet(other, carry):
-        @pl.when(other != me)
-        def _():
-            pl.semaphore_signal(
-                barrier, inc=1, device_id=(other // halves, other % halves), device_id_type=MESH
-            )
-
-        return carry
-
-    lax.fori_loop(0, users * halves, greet, 0)
-
-
-def back_kernel(
-    lengths_ref, own_ref, entry_ref, partial_ref, cot_ref, out_ref,
-    extra, grad, mine, others, extra_sems, sent, got, passed, passed_got,
-):
-    hidden, rows = own_ref.shape
-    users, feat, _ = grad.shape
-    halves = lax.axis_size("seq")
-    col = lax.axis_index("col")
-    seq = lax.axis_index("seq")
-    length = lengths_ref[col]
-    first = seq * rows
-    barrier = pltpu.get_barrier_semaphore()
-    greet_all(barrier, users, halves, col * halves + seq)
-    pl.semaphore_wait(barrier, users * halves - 1)
-
-    extra_copy = pltpu.make_async_remote_copy(
-        src_ref=partial_ref,
-        dst_ref=extra,
-        send_sem=extra_sems.at[0],
-        recv_sem=extra_sems.at[1],
-        device_id=(col, 0),
-        device_id_type=MESH,
-    )
-
-    @pl.when(seq == 1)
-    def _():
-        extra_copy.start()
-
-    def chunk(step, carry):
-        at = pl.ds(pl.multiple_of(step * LANES, LANES), LANES)
-        centered, inverse = column_stats(own_ref[:, at].astype(F32))
-        received = jnp.where(seq == 0, extra[:, at].astype(F32), 0.0)
-        back = norm_back(centered * inverse, inverse, entry_ref[:, at] + received)
-        lane_valid = (
-            lax.broadcasted_iota(jnp.int32, (1, LANES), 1) + first + step * LANES < length
-        )
-        total = jnp.where(lane_valid, turn(cot_ref[at, :]), 0.0) + back
-        grad[:, :, at] = total.reshape(users, feat, LANES).astype(BF16)
-        return carry
-
-    @pl.when(seq == 1)
-    def _():
-        extra[...] = jnp.zeros_like(extra)
-
-    @pl.when(seq == 0)
-    def _():
-        extra_copy.wait_recv()
-
-    lax.fori_loop(0, rows // LANES, chunk, 0)
-
-    def to_owner(user, sender):
-        return pltpu.make_async_remote_copy(
-            src_ref=grad.at[user],
-            dst_ref=mine.at[sender],
-            send_sem=sent.at[user],
-            recv_sem=got.at[sender],
-            device_id=(user, seq),
-            device_id_type=MESH,
-        )
-
-    def to_twin(source, sender):
-        return pltpu.make_async_remote_copy(
-            src_ref=source.at[sender],
-            dst_ref=others.at[sender],
-            send_sem=passed.at[sender],
-            recv_sem=passed_got.at[sender],
-            device_id=(col, 1 - seq),
-            device_id_type=MESH,
-        )
-
-    def send(step, carry):
-        user = lax.rem(col + 1 + step, users)
-        to_owner(user, col).start()
-        return carry
-
-    lax.fori_loop(0, users - 1, send, 0)
-    to_twin(grad, col).start()
-    out_ref[col] = grad[col]
-
-    def forward(step, carry):
-        sender = lax.rem(col + users - 1 - step, users)
-        to_owner(sender, sender).wait_recv()
-        to_twin(mine, sender).start()
-        out_ref[sender] = mine[sender]
-        return carry
-
-    lax.fori_loop(0, users - 1, forward, 0)
-
-    def collect(step, carry):
-        sender = lax.rem(col + users - step, users)
-        to_twin(mine, sender).wait_recv()
-        out_ref[users + sender] = others[sender]
-        return carry
-
-    lax.fori_loop(0, users, collect, 0)
-
-    def leave(step, carry):
-        user = lax.rem(col + 1 + step, users)
-        to_owner(user, col).wait_send()
-        to_twin(mine, user).wait_send()
-        return carry
-
-    lax.fori_loop(0, users - 1, leave, 0)
-    to_twin(grad, col).wait_send()
-
-    @pl.when(seq == 1)
-    def _():
-        extra_copy.wait_send()
-
-
-def send_back(lengths, own, entry, partial, cot, users):
-    hidden, rows = own.shape
-    vmem = pl.BlockSpec(memory_space=pltpu.VMEM)
-    slabs = (users, hidden // users, rows)
-    return pl.pallas_call(
-        back_kernel,
-        out_shape=jax.ShapeDtypeStruct((2 * users,) + slabs[1:], BF16),
-        in_specs=[pl.BlockSpec(memory_space=pltpu.SMEM)] + [vmem] * 4,
-        out_specs=vmem,
-        scratch_shapes=[pltpu.VMEM((hidden, rows), BF16)]
+            pltpu.VMEM((hidden, rows), F32),
+            pltpu.VMEM((hidden, rows), F32),
+            pltpu.VMEM((hidden, rows), BF16),
+            pltpu.VMEM((hidden, rows), BF16),
+        ]
         + [pltpu.VMEM(slabs, BF16)] * 3
         + [pltpu.SemaphoreType.DMA((2,))]
         + [pltpu.SemaphoreType.DMA((users,))] * 4,
         compiler_params=pltpu.CompilerParams(
             vmem_limit_bytes=VMEM_BYTES, collective_id=1, has_side_effects=True
         ),
-        name="send_back",
-    )(lengths, own, entry, partial, cot)
+        name="layer",
+    )(lengths, own, peer, input_weight.T, input_weight, output_weight.T, output_weight, cot)
 
 
 def per_device(history_items, lengths, item_table, input_weight, output_weight, output_cotangent):
@@ -682,8 +660,9 @@
     own = own.reshape(user_count * feat_cols, seq_rows)
     peer = peer.reshape(user_count * feat_cols, seq_rows)
     cot = output_cotangent[0]
-    layer_output, entry, partial = layer(lengths, own, peer, input_weight, output_weight, cot)
-    every_grad = send_back(lengths, own, entry, partial, cot, user_count)
+    layer_output, every_grad = layer(
+        lengths, own, peer, input_weight, output_weight, cot, user_count
+    )
     every_item = jnp.concatenate([history_items, twin_items], axis=0)
     starts = seq_rows * jnp.stack([seq_index, 1 - seq_index])
     counts = jnp.clip(lengths[None, :] - starts[:, None], 0, seq_rows).reshape(-1)

time: 178 us -> 164 us (0.921)
  the two profiles are of different devices: /device:TPU:0 before, /device:TPU:26 now
where the time goes in v3:
time: 164 us; the launch traced here: 162 us
  Pallas kernels  147 us (90%)
  local copies, waits for them, and re-layouts  8.88 us (5%)
  other arithmetic  4.52 us (3%)
    pallas_call x1, Pallas kernels, layer(): pl.pallas_call(layer_kernel, out_shape=(jax.ShapeDtypeStruct((rows, hidde...  75.8 us
    pallas_call x1, Pallas kernels, scatter(): pl.pallas_call(scatter_kernel, out_shape=jax.ShapeDtypeStruct((feat, owne...  36.6 us
    pallas_call x1, Pallas kernels, lookup(): pl.pallas_call(lookup_kernel, out_shape=(jax.ShapeDtypeStruct(slabs, jnp....  35 us
    unnamed x8, local copies, waits for them, and re-layouts  6.12 us

profile of v3, /device:TPU:26, one launch (start us, length us, event | category | flops | bytes accessed | tf_op | source)
XLA Modules:
  0.0 161.5 jit_solution(9592434383887745620)
XLA Ops:
  0.6 0.1 add_multiply_fusion
  0.7 0.7 subtract_clamp_fusion
  1.4 0.6 min.12.count_ref
  2.0 0.8 reshape_dynamic-update-slice_fusion.1
  2.8 1.4 constant_dynamic-update-slice_fusion.1
  4.2 0.6 broadcast_in_dim.6.slot_ref
  4.9 2.0 %copy.9 = bf16[512,512]{0,1:T(8,128)(2,1)} copy(bf16[512,512]{1,0:T(8,128)(2,1)} %out_w_ref.1) | data formatting | bytes 1048576 | tf_op args[4]
  6.9 0.0 copy-start
  6.9 35.0 %lookup.1 = (bf16[16,32,512]{2,1,0:T(8,128)(2,1)}, bf16[16,32,512]{2,1,0:T(8,128)(2,1)}, s32[16,512]{1,0:T(8,128)}) custom-call(s32[16,512]{1,0:T(8,128)} %get-tuple-element.13.rows_ref, s32[16,1,512]{2,1,0:T(1,128)} %broadcast_in_dim.6.slot_ref, f32[32,65536]{1,0:T(8,128)} %table_ref.1, s32[16,512]{1,0:T(8,128)} %items_ref.1), custom_call_target="tpu_custom_call" | custom-call | tf_op jit(solution)/shard_map/lookup/pallas_call | solution.py:176
  42.0 0.8 reshape_dynamic-update-slice_fusion
  42.8 1.6 compare_select_fusion.2.slot_ref
  44.3 0.8 constant_dynamic-update-slice_fusion
  45.1 0.7 fusion.3.rows_ref
  45.8 0.0 copy-done
  45.8 2.5 %copy.8 = bf16[512,2048]{0,1:T(8,128)(2,1)} copy(bf16[512,2048]{1,0:T(8,128)(2,1)S(1)} %copy-done) | data formatting | bytes 4194304 | tf_op args[3]
  48.3 75.8 %layer.1 = (bf16[512,512]{1,0:T(8,128)(2,1)}, bf16[32,32,512]{2,1,0:T(8,128)(2,1)}) custom-call(s32[16]{0:T(128)} %lengths_ref.1, bf16[512,512]{1,0:T(8,128)(2,1)} %bitcast.12, bf16[512,512]{1,0:T(8,128)(2,1)} %bitcast.13, bf16[2048,512]{1,0:T(8,128)(2,1)} %bitcast.8, bf16[512,2048]{1,0:T(8,128)(2,1)} %in_ref.1, bf16[512,512]{1,0:T(8,128)(2,1)} %bitcast.9, ...), custom_call_target="tpu_custom_call" | custom-call | tf_op jit(solution)/shard_map/layer/pallas_call | solution.py:614
  124.1 0.0 copy-start.1
  124.1 36.6 %scatter.1 = f32[32,32768]{1,0:T(8,128)} custom-call(s32[32,512]{1,0:T(8,128)} %fusion.3.rows_ref, s32[32]{0:T(128)} %min.12.count_ref, s32[32,1,512]{2,1,0:T(1,128)} %compare_select_fusion.2.slot_ref, bf16[32,32,512]{2,1,0:T(8,128)(2,1)} %get-tuple-element.11.grad_ref), custom_call_target="tpu_custom_call" | custom-call | tf_op jit(solution)/shard_map/scatter/pallas_call | solution.py:266
  160.7 0.0 copy-done.1
  160.7 0.8 copy.13
Async XLA Ops:
  6.9 38.9 %copy-start = (bf16[512,2048]{1,0:T(8,128)(2,1)S(1)}, bf16[512,2048]{1,0:T(8,128)(2,1)}, u32[]{:S(2)}) copy-start(bf16[512,2048]{1,0:T(8,128)(2,1)} %in_ref.1) | copy-start | bytes 6291460
  124.1 36.6 %copy-start.1 = (bf16[512,512]{1,0:T(8,128)(2,1)S(1)}, bf16[512,512]{1,0:T(8,128)(2,1)}, u32[]{:S(2)}) copy-start(bf16[512,512]{1,0:T(8,128)(2,1)} %get-tuple-element.9) | copy-start | bytes 1572868

commit v4 on v3

--- a/solution.py
+++ b/solution.py
@@ -24,8 +24,8 @@
 
 def packed_place(items, feat):
     groups = LANES // feat
-    row = (items // (LANES * groups)) * LANES + items % LANES
-    slot = (items // LANES) % groups
+    row = ((items >> (LANES * groups).bit_length() - 1) << 7) | (items & (LANES - 1))
+    slot = (items >> 7) & (groups - 1)
     return row, slot
 
 
@@ -43,8 +43,8 @@
 
 
 def lookup_kernel(
-    rows_ref, slot_ref, table_ref, items_ref, own_ref, peer_ref, twin_items_ref,
-    packed, picked, slab, own, peer, twin, own_sent, own_got, peer_sent, peer_got, twin_sems,
+    rows_ref, table_ref, items_ref, own_ref, peer_ref, place_ref, place_slot_ref,
+    packed, picked, slot_ref, slab, own, peer, twin, own_sent, own_got, peer_sent, peer_got, twin_sems,
 ):
     feat, table_cols = table_ref.shape
     users, _, seq_rows = slot_ref.shape
@@ -65,6 +65,9 @@
         return carry
 
     lax.fori_loop(0, table_cols // span, pack, 0, unroll=4)
+    _, slots = packed_place(items_ref[...], feat)
+    for user in range(users):
+        slot_ref[user] = slots[user : user + 1, :]
     pl.semaphore_wait(barrier, users * halves - 1)
     items_copy = pltpu.make_async_remote_copy(
         src_ref=items_ref,
@@ -86,15 +89,20 @@
             device_id_type=MESH,
         )
 
-    def to_peer(user, sender):
+    def to_peer(source, sender):
         return pltpu.make_async_remote_copy(
-            src_ref=slab.at[user],
+            src_ref=source.at[sender],
             dst_ref=peer.at[sender],
-            send_sem=peer_sent.at[user],
+            send_sem=peer_sent.at[sender],
             recv_sem=peer_got.at[sender],
-            device_id=(user, 1),
+            device_id=(col, 1),
             device_id_type=MESH,
         )
+
+    def pass_on(step):
+        sender = lax.rem(col + users - 1 - step, users)
+        to_own(sender, sender).wait_recv()
+        to_peer(own, sender).start()
 
     def one_user(step, carry):
         user = lax.rem(col + 1 + step, users)
@@ -115,24 +123,40 @@
                 total = jnp.where(slot == g, turned[g * feat : (g + 1) * feat, :], total)
             slab[user, :, pl.ds(part * LANES, LANES)] = total.astype(slab.dtype)
 
-        @pl.when(seq == 0)
-        def _():
-            to_peer(user, col).start()
-
         @pl.when(user != col)
         def _():
             to_own(user, col).start()
 
+        @pl.when((seq == 0) & (step >= 2))
+        def _():
+            pass_on(step - 2)
+
         return carry
 
     lax.fori_loop(0, users, one_user, 0)
+
+    @pl.when(seq == 0)
+    def _():
+        to_peer(slab, col).start()
+        pass_on(users - 2)
+
     own_ref[col] = slab[col]
     items_copy.wait()
-    twin_items_ref[...] = twin[...]
+    owned = table_cols // halves
+    for half, ref in enumerate((items_ref, twin)):
+        row, slots = packed_place(ref[...] & (owned - 1), feat)
+        slots = jnp.where(ref[...] >> owned.bit_length() - 1 == seq, slots, -1)
+        place_ref[half * users : (half + 1) * users, :] = row
+        for user in range(users):
+            place_slot_ref[half * users + user] = slots[user : user + 1, :]
 
     def collect(step, carry):
         other = lax.rem(col + 1 + step, users)
-        to_own(other, other).wait_recv()
+
+        @pl.when(seq == 1)
+        def _():
+            to_own(other, other).wait_recv()
+
         own_ref[other] = own[other]
         return carry
 
@@ -141,7 +165,7 @@
     @pl.when(seq == 1)
     def _():
         def collect_peer(other, carry):
-            to_peer(other, other).wait_recv()
+            to_peer(own, other).wait_recv()
             return carry
 
         lax.fori_loop(0, users, collect_peer, 0)
@@ -161,7 +185,7 @@
     @pl.when(seq == 0)
     def _():
         def sent_peer(other, carry):
-            to_peer(other, col).wait_send()
+            to_peer(own, other).wait_send()
             return carry
 
         lax.fori_loop(0, users, sent_peer, 0)
@@ -170,18 +194,22 @@
 def lookup(items, item_table):
     feat, table_cols = item_table.shape
     users, seq_rows = items.shape
-    row, slot = packed_place(items, feat)
+    row, _ = packed_place(items, feat)
     vmem = pl.BlockSpec(memory_space=pltpu.VMEM)
     slabs = (users, feat, seq_rows)
     return pl.pallas_call(
         lookup_kernel,
         out_shape=(jax.ShapeDtypeStruct(slabs, jnp.bfloat16),) * 2
-        + (jax.ShapeDtypeStruct(items.shape, items.dtype),),
-        in_specs=[pl.BlockSpec(memory_space=pltpu.SMEM), vmem, vmem, vmem],
-        out_specs=(vmem,) * 3,
+        + (
+            jax.ShapeDtypeStruct((2 * users, seq_rows), jnp.int32),
+            jax.ShapeDtypeStruct((2 * users, 1, seq_rows), jnp.int32),
+        ),
+        in_specs=[pl.BlockSpec(memory_space=pltpu.SMEM), vmem, vmem],
+        out_specs=(vmem,) * 4,
         scratch_shapes=[
             pltpu.VMEM((table_cols * feat // LANES, LANES), jnp.float32),
             pltpu.VMEM((seq_rows, LANES), jnp.float32),
+            pltpu.VMEM((users, 1, seq_rows), jnp.int32),
             pltpu.VMEM(slabs, jnp.bfloat16),
             pltpu.VMEM(slabs, jnp.bfloat16),
             pltpu.VMEM(slabs, jnp.bfloat16),
@@ -193,10 +221,10 @@
             vmem_limit_bytes=VMEM_BYTES, collective_id=0, has_side_effects=True
         ),
         name="lookup",
-    )(row, slot[:, None], item_table, items)
-
-
-def scatter_kernel(rows_ref, count_ref, slot_ref, grad_ref, out_ref, placed, *sums):
+    )(row, item_table, items)
+
+
+def scatter_kernel(rows_ref, lengths_ref, slot_ref, grad_ref, out_ref, placed, *sums):
     feat, owned = out_ref.shape
     blocks, _, seq_rows = slot_ref.shape
     groups = LANES // feat
@@ -211,7 +239,10 @@
     lax.fori_loop(0, owned // span, clear, 0)
 
     def one_block(block, carry):
-        count = count_ref[block]
+        users = lengths_ref.shape[0]
+        seq = lax.axis_index("seq")
+        start = jnp.where(block < users, seq, 1 - seq) * seq_rows
+        count = jnp.clip(lengths_ref[lax.rem(block, users)] - start, 0, seq_rows)
 
         def place(part, inner):
             at = pl.ds(pl.multiple_of(part * LANES, LANES), LANES)
@@ -257,11 +288,8 @@
     lax.fori_loop(0, owned // span, unpack, 0, unroll=4)
 
 
-def scatter(items, counts, grads, owned, seq_index):
+def scatter(row, slot, lengths, grads, owned):
     feat = grads.shape[1]
-    local = items % owned
-    row, slot = packed_place(local, feat)
-    slot = jnp.where(items // owned == seq_index, slot, -1)
     packed_rows = owned * feat // LANES
     return pl.pallas_call(
         scatter_kernel,
@@ -277,7 +305,7 @@
         + [pltpu.VMEM((packed_rows, LANES), jnp.float32)] * COPIES,
         compiler_params=pltpu.CompilerParams(vmem_limit_bytes=VMEM_BYTES),
         name="scatter",
-    )(row, counts, slot[:, None], grads)
+    )(row, lengths, slot, grads)
 
 
 def dot(left, right):
@@ -369,11 +397,10 @@
     def head_rows(start, head):
         return pl.ds(pl.multiple_of(start + head * DH, DH), DH)
 
-    def weigh(scores):
-        scaled = scores * score_scale
-        sig = sigmoid(scaled)
-        silu = scaled * sig
-        return silu * length_scale, (sig + silu * (1.0 - sig)) * length_scale
+    def weigh(half):
+        above = 1.0 + jnp.tanh(half)
+        silu = half * above
+        return silu, above + silu * (2.0 - above)
 
     below = lax.broadcasted_iota(jnp.int32, (BLOCK, BLOCK), 1) <= lax.broadcasted_iota(
         jnp.int32, (BLOCK, BLOCK), 0
@@ -381,7 +408,7 @@
     blocks = rows // BLOCK
 
     def forward(head, carry):
-        query_rows[head] = turn(act[head_rows(2 * hidden, head), :]).astype(BF16)
+        query_rows[head] = (turn(act[head_rows(2 * hidden, head), :]) * (0.5 * score_scale)).astype(BF16)
         for i in range(blocks):
             at_i = pl.ds(i * BLOCK, BLOCK)
             query = query_rows[head, at_i, :]
@@ -396,7 +423,7 @@
                 point[head, at_i, at_j] = weight
                 bend[head, at_i, at_j] = curve.astype(BF16)
                 total += dot_last(act[head_rows(hidden, head), at_j], weight)
-            att[head_rows(0, head), at_i] = total
+            att[head_rows(0, head), at_i] = total * length_scale
 
         @pl.when(has_peer)
         def _():
@@ -407,7 +434,9 @@
                 weight = weight.astype(BF16)
                 point_peer[head, at_i, :] = weight
                 bend_peer[head, at_i, :] = curve.astype(BF16)
-                att[head_rows(0, head), at_i] += dot_last(act_peer[head_rows(0, head), :], weight)
+                att[head_rows(0, head), at_i] += length_scale * dot_last(
+                    act_peer[head_rows(0, head), :], weight
+                )
 
         return carry
 
@@ -442,7 +471,7 @@
     lax.fori_loop(0, rows // LANES, mix, 0)
 
     def backward_peer(head, carry):
-        grad_rows[head] = turn(grad_cols[head_rows(0, head), :]).astype(BF16)
+        grad_rows[head] = (turn(grad_cols[head_rows(0, head), :]) * (0.5 * length_scale)).astype(BF16)
         value_total = jnp.zeros((DH, rows), F32)
         key_total = jnp.zeros((DH, rows), F32)
         for i in range(blocks):
@@ -454,7 +483,7 @@
             query_grad[head_rows(0, head), at_i] = dot_last(
                 act_peer[head_rows(hidden, head), :], score_grad
             )
-        value_total = jnp.where(valid_peer, value_total, 0.0)
+        value_total = jnp.where(valid_peer, value_total * length_scale, 0.0)
         pre_grad_peer[head_rows(0, head), :] = (
             value_total * slope_peer[head_rows(0, head), :]
         ).astype(BF16)
@@ -490,7 +519,7 @@
     @pl.when(jnp.logical_not(has_peer))
     def _():
         def rows_only(head, carry):
-            grad_rows[head] = turn(grad_cols[head_rows(0, head), :]).astype(BF16)
+            grad_rows[head] = (turn(grad_cols[head_rows(0, head), :]) * (0.5 * length_scale)).astype(BF16)
             return carry
 
         lax.fori_loop(0, H, rows_only, 0)
@@ -513,7 +542,7 @@
             pre_grad[query_at, at_i] = (query_total * score_scale * slope[query_at, at_i]).astype(
                 BF16
             )
-        value_total = jnp.where(valid, jnp.concatenate(value_parts, axis=1), 0.0)
+        value_total = jnp.where(valid, jnp.concatenate(value_parts, axis=1) * length_scale, 0.0)
         key_total = jnp.concatenate(key_parts, axis=1) * score_scale
         for start, total in ((hidden, value_total), (3 * hidden, key_total)):
             at = head_rows(start, head)
@@ -655,19 +684,15 @@
 def per_device(history_items, lengths, item_table, input_weight, output_weight, output_cotangent):
     user_count, seq_rows = history_items.shape
     feat_cols = item_table.shape[0]
-    seq_index = lax.axis_index("seq")
-    own, peer, twin_items = lookup(history_items, item_table)
+    own, peer, row, slot = lookup(history_items, item_table)
     own = own.reshape(user_count * feat_cols, seq_rows)
     peer = peer.reshape(user_count * feat_cols, seq_rows)
     cot = output_cotangent[0]
     layer_output, every_grad = layer(
         lengths, own, peer, input_weight, output_weight, cot, user_count
     )
-    every_item = jnp.concatenate([history_items, twin_items], axis=0)
-    starts = seq_rows * jnp.stack([seq_index, 1 - seq_index])
-    counts = jnp.clip(lengths[None, :] - starts[:, None], 0, seq_rows).reshape(-1)
     owned_rows = item_table.shape[1] // lax.axis_size("seq")
-    table_gradient = scatter(every_item, counts, every_grad, owned_rows, seq_index)
+    table_gradient = scatter(row, slot, lengths, every_grad, owned_rows)
     return (layer_output[None], table_gradient)
 
 

time: 164 us -> 155 us (0.945)
  the two profiles are of different devices: /device:TPU:26 before, /device:TPU:0 now
where the time goes in v4:
time: 155 us; the launch traced here: 153 us
  Pallas kernels  145 us (94%)
  local copies, waits for them, and re-layouts  5.35 us (3%)
    pallas_call x1, Pallas kernels, layer(): pl.pallas_call(layer_kernel, out_shape=(jax.ShapeDtypeStruct((rows, hidde...  66.4 us
    pallas_call x1, Pallas kernels, lookup(): pl.pallas_call(lookup_kernel, out_shape=(jax.ShapeDtypeStruct(slabs, jnp....  40.4 us
    pallas_call x1, Pallas kernels, scatter(): pl.pallas_call(scatter_kernel, out_shape=jax.ShapeDtypeStruct((feat, owne...  38.6 us
    unnamed x7, local copies, waits for them, and re-layouts  5.35 us

profile of v4, /device:TPU:0, one launch (start us, length us, event | category | flops | bytes accessed | tf_op | source)
XLA Modules:
  0.0 152.7 jit_solution(12881975424028831666)
XLA Ops:
  0.6 1.4 and_or_fusion.rows_ref
  2.0 2.0 %copy.9 = bf16[512,512]{0,1:T(8,128)(2,1)} copy(bf16[512,512]{1,0:T(8,128)(2,1)} %out_w_ref.1) | data formatting | bytes 1048576 | tf_op args[4]
  4.1 0.0 copy-start
  4.1 40.4 %lookup.1 = (bf16[16,32,512]{2,1,0:T(8,128)(2,1)}, bf16[16,32,512]{2,1,0:T(8,128)(2,1)}, s32[32,512]{1,0:T(8,128)}, s32[32,1,512]{2,1,0:T(1,128)}) custom-call(s32[16,512]{1,0:T(8,128)} %and_or_fusion.rows_ref, f32[32,65536]{1,0:T(8,128)} %table_ref.1, s32[16,512]{1,0:T(8,128)} %items_ref.1), custom_call_target="tpu_custom_call" | custom-call | tf_op jit(solution)/shard_map/lookup/pallas_call | solution.py:200
  44.5 0.0 copy-done
  44.5 2.5 %copy.8 = bf16[512,2048]{0,1:T(8,128)(2,1)} copy(bf16[512,2048]{1,0:T(8,128)(2,1)S(1)} %copy-done) | data formatting | bytes 4194304 | tf_op args[3]
  47.0 66.4 %layer.1 = (bf16[512,512]{1,0:T(8,128)(2,1)}, bf16[32,32,512]{2,1,0:T(8,128)(2,1)}) custom-call(s32[16]{0:T(128)} %lengths_ref.3, bf16[512,512]{1,0:T(8,128)(2,1)} %bitcast.10, bf16[512,512]{1,0:T(8,128)(2,1)} %bitcast.11, bf16[2048,512]{1,0:T(8,128)(2,1)} %bitcast.6, bf16[512,2048]{1,0:T(8,128)(2,1)} %in_ref.1, bf16[512,512]{1,0:T(8,128)(2,1)} %bitcast.7, ...), custom_call_target="tpu_custom_call" | custom-call | tf_op jit(solution)/shard_map/layer/pallas_call | solution.py:643
  113.4 0.0 copy-start.1
  113.4 38.6 %scatter.1 = f32[32,32768]{1,0:T(8,128)} custom-call(s32[32,512]{1,0:T(8,128)} %get-tuple-element.11.rows_ref, s32[16]{0:T(128)} %lengths_ref.3, s32[32,1,512]{2,1,0:T(1,128)} %get-tuple-element.12.slot_ref, bf16[32,32,512]{2,1,0:T(8,128)(2,1)} %get-tuple-element.13.grad_ref), custom_call_target="tpu_custom_call" | custom-call | tf_op jit(solution)/shard_map/scatter/pallas_call | solution.py:294
  151.9 0.0 copy-done.1
  152.0 0.8 copy.11
Async XLA Ops:
  4.1 40.4 %copy-start = (bf16[512,2048]{1,0:T(8,128)(2,1)S(1)}, bf16[512,2048]{1,0:T(8,128)(2,1)}, u32[]{:S(2)}) copy-start(bf16[512,2048]{1,0:T(8,128)(2,1)} %in_ref.1) | copy-start | bytes 6291460
  113.4 38.6 %copy-start.1 = (bf16[512,512]{1,0:T(8,128)(2,1)S(1)}, bf16[512,512]{1,0:T(8,128)(2,1)}, u32[]{:S(2)}) copy-start(bf16[512,512]{1,0:T(8,128)(2,1)} %get-tuple-element.10) | copy-start | bytes 1572868

commit v5 on v4

--- a/solution.py
+++ b/solution.py
@@ -337,7 +337,7 @@
 
 
 def layer_kernel(
-    lengths_ref, own_ref, peer_ref, in_turned_ref, in_ref, out_turned_ref, out_w_ref, cot_ref,
+    lengths_ref, own_ref, peer_ref, in_ref, out_turned_ref, out_w_ref, cot_ref,
     out_ref, back_ref,
     normed, act, slope, act_peer, slope_peer, query_rows, att, scale, gated, grad_cols, grad_rows,
     point, bend, point_peer, bend_peer, pre_grad, pre_grad_peer, query_grad,
@@ -372,7 +372,9 @@
         def tile(step, carry):
             source = pl.ds(pl.multiple_of(from_row + step * BLOCK, BLOCK), BLOCK)
             target = pl.ds(pl.multiple_of(to_row + step * BLOCK, BLOCK), BLOCK)
-            pre = dot(in_turned_ref[source, :], normed[...])
+            pre = lax.dot_general(
+                in_ref[:, source], normed[...], (((0,), (0,)), ((), ())), preferred_element_type=F32
+            )
             sig = sigmoid(pre)
             result = pre * sig
             if keep is not None:
@@ -646,7 +648,7 @@
             jax.ShapeDtypeStruct((rows, hidden), BF16),
             jax.ShapeDtypeStruct((2 * users,) + slabs[1:], BF16),
         ),
-        in_specs=[pl.BlockSpec(memory_space=pltpu.SMEM)] + [vmem] * 7,
+        in_specs=[pl.BlockSpec(memory_space=pltpu.SMEM)] + [vmem] * 6,
         out_specs=(vmem,) * 2,
         scratch_shapes=[
             pltpu.VMEM((hidden, rows), BF16),
@@ -678,7 +680,7 @@
             vmem_limit_bytes=VMEM_BYTES, collective_id=1, has_side_effects=True
         ),
         name="layer",
-    )(lengths, own, peer, input_weight.T, input_weight, output_weight.T, output_weight, cot)
+    )(lengths, own, peer, input_weight, output_weight.T, output_weight, cot)
 
 
 def per_device(history_items, lengths, item_table, input_weight, output_weight, output_cotangent):

time: 155 us -> 157 us (1.013); the launches traced: 153 us -> 158 us
  Pallas kernels: 145 us -> 153 us
  local copies, waits for them, and re-layouts: 5.35 us -> 2.84 us
    pallas_call x1, Pallas kernels: 38.6 us -> 46.3 us  [scatter(): pl.pallas_call(scatter_kernel, out_shape=jax.ShapeDtypeStruct((feat, owne...]
    unnamed x7 -> x4, local copies, waits for them, and re-layouts: 5.35 us -> 2.84 us
where the time goes in v5:
time: 157 us; the launch traced here: 158 us
  Pallas kernels  153 us (97%)
  local copies, waits for them, and re-layouts  2.84 us (2%)
    pallas_call x1, Pallas kernels, layer(): pl.pallas_call(layer_kernel, out_shape=(jax.ShapeDtypeStruct((rows, hidde...  66.2 us
    pallas_call x1, Pallas kernels, scatter(): pl.pallas_call(scatter_kernel, out_shape=jax.ShapeDtypeStruct((feat, owne...  46.3 us
    pallas_call x1, Pallas kernels, lookup(): pl.pallas_call(lookup_kernel, out_shape=(jax.ShapeDtypeStruct(slabs, jnp....  40.3 us

profile of v5, /device:TPU:0, one launch (start us, length us, event | category | flops | bytes accessed | tf_op | source)
XLA Modules:
  0.0 157.7 jit_solution(2815381014717044505)
XLA Ops:
  0.6 1.4 and_or_fusion.rows_ref
  2.0 2.0 %copy.8 = bf16[512,512]{0,1:T(8,128)(2,1)} copy(bf16[512,512]{1,0:T(8,128)(2,1)} %out_w_ref.1) | data formatting | bytes 1048576 | tf_op args[4]
  4.1 40.3 %lookup.1 = (bf16[16,32,512]{2,1,0:T(8,128)(2,1)}, bf16[16,32,512]{2,1,0:T(8,128)(2,1)}, s32[32,512]{1,0:T(8,128)}, s32[32,1,512]{2,1,0:T(1,128)}) custom-call(s32[16,512]{1,0:T(8,128)} %and_or_fusion.rows_ref, f32[32,65536]{1,0:T(8,128)} %table_ref.1, s32[16,512]{1,0:T(8,128)} %items_ref.1), custom_call_target="tpu_custom_call" | custom-call | tf_op jit(solution)/shard_map/lookup/pallas_call | solution.py:200
  44.3 66.2 %layer.1 = (bf16[512,512]{1,0:T(8,128)(2,1)}, bf16[32,32,512]{2,1,0:T(8,128)(2,1)}) custom-call(s32[16]{0:T(128)} %lengths_ref.3, bf16[512,512]{1,0:T(8,128)(2,1)} %bitcast.7, bf16[512,512]{1,0:T(8,128)(2,1)} %bitcast.8, bf16[512,2048]{1,0:T(8,128)(2,1)} %in_ref.1, bf16[512,512]{1,0:T(8,128)(2,1)} %bitcast.5, bf16[512,512]{1,0:T(8,128)(2,1)} %out_w_ref.1, ...), custom_call_target="tpu_custom_call" | custom-call | tf_op jit(solution)/shard_map/layer/pallas_call | solution.py:645
  110.6 0.0 copy-start
  110.6 46.3 %scatter.1 = f32[32,32768]{1,0:T(8,128)} custom-call(s32[32,512]{1,0:T(8,128)} %get-tuple-element.11.rows_ref, s32[16]{0:T(128)} %lengths_ref.3, s32[32,1,512]{2,1,0:T(1,128)} %get-tuple-element.12.slot_ref, bf16[32,32,512]{2,1,0:T(8,128)(2,1)} %get-tuple-element.13.grad_ref), custom_call_target="tpu_custom_call" | custom-call | tf_op jit(solution)/shard_map/scatter/pallas_call | solution.py:294
  156.9 0.0 copy-done
  156.9 0.8 copy.10
Async XLA Ops:
  110.6 46.3 %copy-start = (bf16[512,512]{1,0:T(8,128)(2,1)S(1)}, bf16[512,512]{1,0:T(8,128)(2,1)}, u32[]{:S(2)}) copy-start(bf16[512,512]{1,0:T(8,128)(2,1)} %get-tuple-element.10) | copy-start | bytes 1572868
